TPU v7x, 512 devices: a whole 4x8x8 slice. The times are simulated.
512 devices in a mesh: ctx: 64 (over z, y_lo, x), seq: 8 (over y_hi, core).
Axes of the slice: x: 4, y: 8 (y_hi: 4, y_lo: 2; y = y_hi * 2 + y_lo), z: 8, core: 2. Of those that a mesh axis runs over, the one named last changes fastest.
Arguments:
- queries: bfloat16 [65536, 4096], P(('seq', 'ctx')), parts along dimension 0, may hold values from -140 to 140
- keys: bfloat16 [65536, 512], P(('seq', 'ctx')), parts along dimension 0, may hold values from -7 to 7
- values: bfloat16 [65536, 512], P(('seq', 'ctx')), parts along dimension 0, may hold values from -6 to 6
- key_value_scales: float32 [2048, 2, 4], P('seq'), parts along dimension 0, may hold values from 0.5 to 2
- doc_lengths: int32 [256], P('seq'), parts along dimension 0, may hold values from 1 to 512, 8192 in all
Outputs:
- attended: bfloat16 [65536, 4096], P(('seq', 'ctx')), parts along dimension 0
There are 8 independent parts, one for each index of `seq`. A program takes and returns all parts, laid end to end along the dimension named above; each array names one. Nothing has to cross between parts.
Inputs may be any that keep to these rules, and one draw needn't show every extreme that they name: doc_lengths sum to 8192; each is at most 512.
All inputs are finite; a program needn't handle non-finite values.
Results may differ from a plain program's by a relative error of at most 0.0047.
Values may be sent and summed in bfloat16 or wider, within the bound.
No kernel may reach another device: no remote copies, remote signals or barrier semaphores. Data moves between devices by JAX's collectives and lax.ppermute only.
A program may use at most 64 MiB of HBM per device.

v0:
```python
import math

import jax
import jax.numpy as jnp
from jax import lax
from jax.sharding import PartitionSpec as P

SCALE_BLOCK = 32
REACH = 4


def shifted(block, axis, distance):
    devices = range(lax.axis_size(axis))
    route = [(i - distance, i) for i in devices if i - distance in devices]
    return lax.ppermute(block, axis, route)


def attend_tile(state, qview, kblock, vblock, scales, qpos, kpos, qstart_of, inverse):
    best, total, accum = state
    mask = (kpos[None, :] >= qstart_of[:, None]) & (kpos[None, :] <= qpos[:, None])
    score = jnp.einsum("tgjd,sgd->tgjs", qview, kblock, preferred_element_type=jnp.float32)
    score = score * (scales[:, 0, :].T * inverse)[None, :, None, :]
    score = jnp.where(mask[:, None, None, :], score, -jnp.inf)
    fresh = jnp.maximum(best, jnp.max(score, axis=-1))
    prob = jnp.exp(score - fresh[..., None])
    factor = jnp.exp(best - fresh)
    total = total * factor + jnp.sum(prob, axis=-1)
    weighted = (prob * scales[:, 1, :].T[None, :, None, :]).astype(jnp.bfloat16)
    accum = accum * factor[..., None] + jnp.einsum(
        "tgjs,sgd->tgjd", weighted, vblock, preferred_element_type=jnp.float32
    )
    return (fresh, total, accum)


def per_device(queries, keys, values, key_value_scales, doc_lengths):
    rows = queries.shape[0]
    groups = key_value_scales.shape[2]
    head = keys.shape[1] // groups
    qheads = queries.shape[1] // head
    inverse = 1.0 / math.sqrt(head)
    first = lax.axis_index("ctx") * rows
    qpos = first + jnp.arange(rows, dtype=jnp.int32)
    ends = jnp.cumsum(doc_lengths)
    qstart_of = jnp.sum(jnp.where(ends[None, :] <= qpos[:, None], doc_lengths[None, :], 0), axis=1)
    qview = queries.reshape(rows, groups, qheads // groups, head)
    shape_stat = (rows, groups, qheads // groups)
    state = (
        jnp.full(shape_stat, -jnp.inf, jnp.float32),
        jnp.zeros(shape_stat, jnp.float32),
        jnp.zeros(shape_stat + (head,), jnp.float32),
    )

    def visit(state, kflat, vflat, back):
        kfirst = first - back * rows
        kpos = kfirst + jnp.arange(rows, dtype=jnp.int32)
        piece = lax.dynamic_slice_in_dim(
            key_value_scales, jnp.maximum(kfirst, 0) // SCALE_BLOCK, rows // SCALE_BLOCK, 0
        )
        scales = jnp.repeat(piece, SCALE_BLOCK, axis=0)
        kblock = kflat.reshape(rows, groups, head)
        vblock = vflat.reshape(rows, groups, head)
        return attend_tile(state, qview, kblock, vblock, scales, qpos, kpos, qstart_of, inverse)

    state = visit(state, keys, values, 0)
    moving = (keys, values)
    for back in range(1, REACH + 1):
        moving = shifted((moving[0], moving[1]), "ctx", 1)
        state = visit(state, moving[0], moving[1], back)
    best, total, accum = state
    result = accum / total[..., None]
    return result.reshape(rows, qheads * head).astype(jnp.bfloat16)


def solution(mesh):
    return jax.shard_map(
        per_device,
        mesh=mesh,
        in_specs=(
            P(("seq", "ctx"), None),
            P(("seq", "ctx"), None),
            P(("seq", "ctx"), None),
            P("seq", None, None),
            P("seq"),
        ),
        out_specs=P(("seq", "ctx"), None),
        check_vma=False,
    )
```

profile of v0, /device:TPU:238, one launch (start us, length us, event | category | flops | bytes accessed | tf_op | source)
XLA Modules:
  0.0 76.0 jit_solution(1326765905116598475)
XLA Ops:
  0.0 1.0 %copy.52 = bf16[128,512]{0,1:T(8,128)(2,1)S(1)} copy(bf16[128,512]{1,0:T(8,128)(2,1)} %param.6) | data formatting | bytes 262144 | tf_op args[1]
  1.0 6.2 %collective-permute-start = (bf16[128,512]{0,1:T(8,128)(2,1)S(1)}, bf16[128,512]{0,1:T(8,128)(2,1)S(1)}, u32[]{:S(2)}, u32[]{:S(2)}) collective-permute-start(bf16[128,512]{0,1:T(8,128)(2,1)S(1)} %copy.52), channel_id=1, source_target_pairs={{0,8},{8,16},{16,24},{24,32},{32,40},{40,48},{48,56},{56,64},{64,7... | collective-permute-start | bytes 393224 | tf_op jit(solution)/shard_map/ppermute | solution.py:15
  7.2 3.4 %collective-permute-start.1 = (bf16[128,512]{1,0:T(8,128)(2,1)}, bf16[128,512]{1,0:T(8,128)(2,1)}, u32[]{:S(2)}, u32[]{:S(2)}) collective-permute-start(bf16[128,512]{1,0:T(8,128)(2,1)} %param.7), channel_id=1, source_target_pairs={{0,8},{8,16},{16,24},{24,32},{32,40},{40,48},{48,56},{56,64},{64,7... | collective-permute-start | bytes 393224 | tf_op jit(solution)/shard_map/ppermute | solution.py:15
  11.7 1.0 %copy.87 = bf16[128,512]{0,1:T(8,128)(2,1)S(1)} copy(bf16[128,512]{1,0:T(8,128)(2,1)} %param.7) | data formatting | bytes 262144 | tf_op jit(solution)/shard_map/reshape | solution.py:61
  15.4 1.4 %copy.96 = bf16[16,8,32,128]{3,2,1,0:T(8,128)(2,1)S(1)} copy(bf16[16,8,32,128]{3,1,2,0:T(8,128)(2,1)} %bitcast.155) | data formatting | bytes 2097152
  20.8 1.9 %fusion.11 = f32[4,128,8,128]{1,3,2,0:T(8,128)} fusion(bf16[128,4,128,1]{0,2,3,1:T(8,128)(2,1)S(1)} %bitcast.157, f32[128,4,8,128]{0,3,2,1:T(8,128)S(1)} %get-tuple-element.42, f32[4,128]{1,0:T(4,128)S(1)} %get-tuple-element.22, f32[128,4,8]{0,2,1:T(8,128)S(1)} %get-tuple-element.41), kind=kOutput, calls=%fused_computation.31 | convolution fusion | flops 135790592 | bytes 4343808 | tf_op jit(solution)/shard_map/tgjs,sgd->tgjd/dot_general | solution.py:29
  23.7 3.4 %collective-permute-start.2 = (bf16[128,512]{0,1:T(8,128)(2,1)S(1)}, bf16[128,512]{0,1:T(8,128)(2,1)S(1)}, u32[]{:S(2)}, u32[]{:S(2)}) collective-permute-start(bf16[128,512]{0,1:T(8,128)(2,1)S(1)} %collective-permute-done), channel_id=1, source_target_pairs={{0,8},{8,16},{16,24},{24,32},{32,40},{40,48},{48,56},{56,64},{64,7... | collective-permute-start | bytes 393224 | tf_op jit(solution)/shard_map/ppermute | solution.py:15
  27.1 1.2 %fusion.41 = (f32[128,4,8]{0,2,1:T(8,128)}, f32[128,4,8,128]{0,3,2,1:T(8,128)S(1)}) fusion(f32[4,128]{1,0:T(4,128)S(1)} %get-tuple-element.25, bf16[128,4,128,1]{0,2,3,1:T(8,128)(2,1)S(1)} %bitcast.162, bf16[128,4,8,128]{3,2,1,0:T(8,128)(2,1)S(1)} %bitcast.151, pred[128,128]{0,1:T(8,128)(4,1)S(1)} %get-tuple-element.30), kind=kOutput, calls=%fused_computation.93 | convolution fusion | flops 135786496 | bytes 3311616 | tf_op jit(solution)/shard_map/tgjd,sgd->tgjs/dot_general | solution.py:21
  28.3 1.0 %copy.55 = bf16[128,512]{0,1:T(8,128)(2,1)S(1)} copy(bf16[128,512]{1,0:T(8,128)(2,1)} %collective-permute-done.1) | data formatting | bytes 262144 | tf_op jit(solution)/shard_map/ppermute | solution.py:15
  29.3 3.1 %collective-permute-start.3 = (bf16[128,512]{1,0:T(8,128)(2,1)}, bf16[128,512]{1,0:T(8,128)(2,1)}, u32[]{:S(2)}, u32[]{:S(2)}) collective-permute-start(bf16[128,512]{1,0:T(8,128)(2,1)} %collective-permute-done.1), channel_id=1, source_target_pairs={{0,8},{8,16},{16,24},{24,32},{32,40},{40,48},{48,56},{56,64},{64,7... | collective-permute-start | bytes 393224 | tf_op jit(solution)/shard_map/ppermute | solution.py:15
  32.5 5.7 %collective-permute-start.4 = (bf16[128,512]{0,1:T(8,128)(2,1)S(1)}, bf16[128,512]{0,1:T(8,128)(2,1)}, u32[]{:S(2)}, u32[]{:S(2)}) collective-permute-start(bf16[128,512]{0,1:T(8,128)(2,1)S(1)} %collective-permute-done.2), channel_id=1, source_target_pairs={{0,8},{8,16},{16,24},{24,32},{32,40},{40,48},{48,56},{56,64},{64,7... | collective-permute-start | bytes 393224 | tf_op jit(solution)/shard_map/ppermute | solution.py:15
  38.1 3.3 %fusion.39 = (f32[128,4,8]{0,2,1:T(8,128)}, f32[128,4,8,128]{0,3,2,1:T(8,128)}) fusion(f32[4,128]{1,0:T(4,128)} %get-tuple-element.27, bf16[128,4,128,1]{0,2,3,1:T(8,128)(2,1)S(1)} %bitcast.163, bf16[128,4,8,128]{3,2,1,0:T(8,128)(2,1)S(1)} %bitcast.152, pred[128,128]{0,1:T(8,128)(4,1)} %get-tuple-element.31), kind=kOutput, calls=%fused_computation.91 | convolution fusion | flops 135786496 | bytes 3311616 | tf_op jit(solution)/shard_map/tgjd,sgd->tgjs/dot_general | solution.py:21
  42.4 2.5 %collective-permute-start.5 = (bf16[128,512]{1,0:T(8,128)(2,1)}, bf16[128,512]{1,0:T(8,128)(2,1)}, u32[]{:S(2)}, u32[]{:S(2)}) collective-permute-start(bf16[128,512]{1,0:T(8,128)(2,1)} %collective-permute-done.3), channel_id=1, source_target_pairs={{0,8},{8,16},{16,24},{24,32},{32,40},{40,48},{48,56},{56,64},{64,7... | collective-permute-start | bytes 393224 | tf_op jit(solution)/shard_map/ppermute | solution.py:15
  44.9 4.4 %collective-permute-start.6 = (bf16[128,512]{0,1:T(8,128)(2,1)}, bf16[128,512]{0,1:T(8,128)(2,1)}, u32[]{:S(2)}, u32[]{:S(2)}) collective-permute-start(bf16[128,512]{0,1:T(8,128)(2,1)} %collective-permute-done.4), channel_id=1, source_target_pairs={{0,8},{8,16},{16,24},{24,32},{32,40},{40,48},{48,56},{56,64},{64,7... | collective-permute-start | bytes 393224 | tf_op jit(solution)/shard_map/ppermute | solution.py:15
  49.3 3.5 %fusion.38 = (f32[128,4,8]{0,2,1:T(8,128)}, f32[128,4,8,128]{0,3,2,1:T(8,128)}) fusion(f32[4,128]{1,0:T(4,128)} %get-tuple-element.29, bf16[128,4,128,1]{0,2,3,1:T(8,128)(2,1)} %bitcast.73, bf16[128,4,8,128]{3,2,1,0:T(8,128)(2,1)S(1)} %bitcast.153, pred[128,128]{0,1:T(8,128)(4,1)} %get-tuple-element.32), kind=kOutput, calls=%fused_computation.90 | convolution fusion | flops 135786496 | bytes 3311616 | tf_op jit(solution)/shard_map/tgjd,sgd->tgjs/dot_general | solution.py:21
  53.9 4.6 %collective-permute-start.7 = (bf16[128,512]{1,0:T(8,128)(2,1)}, bf16[128,512]{1,0:T(8,128)(2,1)}, u32[]{:S(2)}, u32[]{:S(2)}) collective-permute-start(bf16[128,512]{1,0:T(8,128)(2,1)} %collective-permute-done.5), channel_id=1, source_target_pairs={{0,8},{8,16},{16,24},{24,32},{32,40},{40,48},{48,56},{56,64},{64,7... | collective-permute-start | bytes 393224 | tf_op jit(solution)/shard_map/ppermute | solution.py:15
  58.5 1.7 %fusion.37 = (f32[128,4,8]{0,2,1:T(8,128)S(1)}, f32[128,4,8,128]{0,3,2,1:T(8,128)S(1)}) fusion(f32[4,128]{1,0:T(4,128)} %get-tuple-element.21, bf16[128,4,128,1]{0,2,3,1:T(8,128)(2,1)} %bitcast.79, bf16[128,4,8,128]{3,2,1,0:T(8,128)(2,1)S(1)} %bitcast.154, pred[128,128]{0,1:T(8,128)(4,1)} %get-tuple-element.33), kind=kOutput, calls=%fused_computation.89 | convolution fusion | flops 135786496 | bytes 3311616 | tf_op jit(solution)/shard_map/tgjd,sgd->tgjs/dot_general | solution.py:21
  61.6 1.0 %copy-done = f32[128,4,8,128]{0,3,2,1:T(8,128)S(1)} copy-done((f32[128,4,8,128]{0,3,2,1:T(8,128)S(1)}, f32[128,4,8,128]{0,3,2,1:T(8,128)}, u32[]{:S(2)}) %copy-start) | copy-done | bytes 2097176
  63.4 1.8 %fusion.12 = f32[4,128,8,128]{1,3,2,0:T(8,128)} fusion(bf16[128,4,128,1]{0,2,3,1:T(8,128)(2,1)S(1)} %bitcast.159, f32[128,4,8,128]{0,3,2,1:T(8,128)S(1)} %get-tuple-element.44, f32[4,128]{1,0:T(4,128)S(1)} %copy-done.11, f32[128,4,8]{0,2,1:T(8,128)S(1)} %get-tuple-element.13), kind=kOutput, calls=%fused_computation.32 | convolution fusion | flops 135790592 | bytes 4343808 | tf_op jit(solution)/shard_map/tgjs,sgd->tgjd/dot_general | solution.py:29
  65.2 1.9 %fusion.13 = f32[4,128,8,128]{1,3,2,0:T(8,128)} fusion(bf16[128,4,128,1]{0,2,3,1:T(8,128)(2,1)S(1)} %bitcast.160, f32[128,4,8,128]{0,3,2,1:T(8,128)S(1)} %copy-done, f32[4,128]{1,0:T(4,128)S(1)} %copy-done.10, f32[128,4,8]{0,2,1:T(8,128)S(1)} %get-tuple-element.12), kind=kOutput, calls=%fused_computation.33 | convolution fusion | flops 135790592 | bytes 4343808 | tf_op jit(solution)/shard_map/tgjs,sgd->tgjd/dot_general | solution.py:29
  67.1 1.9 %fusion.14 = f32[4,128,8,128]{1,3,2,0:T(8,128)} fusion(bf16[128,4,128,1]{0,2,3,1:T(8,128)(2,1)S(1)} %bitcast.161, f32[128,4,8,128]{0,3,2,1:T(8,128)S(1)} %copy-done.1, f32[4,128]{1,0:T(4,128)S(1)} %copy-done.9, f32[128,4,8]{0,2,1:T(8,128)S(1)} %get-tuple-element.11), kind=kOutput, calls=%fused_computation.34 | convolution fusion | flops 135790592 | bytes 4343808 | tf_op jit(solution)/shard_map/tgjs,sgd->tgjd/dot_general | solution.py:29
  69.0 1.0 %copy.67 = bf16[128,512]{0,1:T(8,128)(2,1)S(1)} copy(bf16[128,512]{1,0:T(8,128)(2,1)} %collective-permute-done.7) | data formatting | bytes 262144 | tf_op jit(solution)/shard_map/ppermute | solution.py:15
  70.1 4.7 %fusion.1 = bf16[128,4,8,128]{0,3,2,1:T(8,128)(2,1)S(1)} fusion(f32[4,128,8,128]{1,3,2,0:T(8,128)} %fusion.14, f32[4,128,8,128]{1,3,2,0:T(8,128)} %fusion.13, f32[4,128,8,128]{1,3,2,0:T(8,128)} %fusion.12, f32[4,128,8,128]{1,3,2,0:T(8,128)} %fusion.11, bf16[128,4,128,1]{0,2,3,1:T(8,128)(2,1)S(1)} %bitcast.164, f32[128,4,8,128]{0,3,2,1:T(8,128)S(1)} %copy-done.3, ...), kind=kOutput, calls=%fused_computation.2 | convolution fusion | flops 141557760 | bytes 11782144 | tf_op jit(solution)/shard_map/tgjs,sgd->tgjd/dot_general | solution.py:29
  74.7 1.3 %copy.69 = bf16[128,4096]{1,0:T(8,128)(2,1)} copy(bf16[128,4096]{0,1:T(8,128)(2,1)S(1)} %bitcast.156) | data formatting | bytes 2097152 | tf_op jit(solution)/shard_map/convert_element_type | solution.py:71
  (70 shorter events, 12.6 us)
Async XLA Ops:
  0.0 19.3 %copy-start.12 = (s32[32]{0:T(128)S(1)}, s32[32]{0:T(128)}, u32[]{:S(2)}) copy-start(s32[32]{0:T(128)} %param.9) | copy-start | bytes 388
  1.0 22.6 %collective-permute-start = (bf16[128,512]{0,1:T(8,128)(2,1)S(1)}, bf16[128,512]{0,1:T(8,128)(2,1)S(1)}, u32[]{:S(2)}, u32[]{:S(2)}) collective-permute-start(bf16[128,512]{0,1:T(8,128)(2,1)S(1)} %copy.52), channel_id=1, source_target_pairs={{0,8},{8,16},{16,24},{24,32},{32,40},{40,48},{48,56},{56,64},{64,7... | collective-permute-start | bytes 393224 | tf_op jit(solution)/shard_map/ppermute | solution.py:15
  7.2 21.1 %collective-permute-start.1 = (bf16[128,512]{1,0:T(8,128)(2,1)}, bf16[128,512]{1,0:T(8,128)(2,1)}, u32[]{:S(2)}, u32[]{:S(2)}) collective-permute-start(bf16[128,512]{1,0:T(8,128)(2,1)} %param.7), channel_id=1, source_target_pairs={{0,8},{8,16},{16,24},{24,32},{32,40},{40,48},{48,56},{56,64},{64,7... | collective-permute-start | bytes 393224 | tf_op jit(solution)/shard_map/ppermute | solution.py:15
  23.7 8.8 %collective-permute-start.2 = (bf16[128,512]{0,1:T(8,128)(2,1)S(1)}, bf16[128,512]{0,1:T(8,128)(2,1)S(1)}, u32[]{:S(2)}, u32[]{:S(2)}) collective-permute-start(bf16[128,512]{0,1:T(8,128)(2,1)S(1)} %collective-permute-done), channel_id=1, source_target_pairs={{0,8},{8,16},{16,24},{24,32},{32,40},{40,48},{48,56},{56,64},{64,7... | collective-permute-start | bytes 393224 | tf_op jit(solution)/shard_map/ppermute | solution.py:15
  29.3 12.1 %collective-permute-start.3 = (bf16[128,512]{1,0:T(8,128)(2,1)}, bf16[128,512]{1,0:T(8,128)(2,1)}, u32[]{:S(2)}, u32[]{:S(2)}) collective-permute-start(bf16[128,512]{1,0:T(8,128)(2,1)} %collective-permute-done.1), channel_id=1, source_target_pairs={{0,8},{8,16},{16,24},{24,32},{32,40},{40,48},{48,56},{56,64},{64,7... | collective-permute-start | bytes 393224 | tf_op jit(solution)/shard_map/ppermute | solution.py:15
  32.5 12.4 %collective-permute-start.4 = (bf16[128,512]{0,1:T(8,128)(2,1)S(1)}, bf16[128,512]{0,1:T(8,128)(2,1)}, u32[]{:S(2)}, u32[]{:S(2)}) collective-permute-start(bf16[128,512]{0,1:T(8,128)(2,1)S(1)} %collective-permute-done.2), channel_id=1, source_target_pairs={{0,8},{8,16},{16,24},{24,32},{32,40},{40,48},{48,56},{56,64},{64,7... | collective-permute-start | bytes 393224 | tf_op jit(solution)/shard_map/ppermute | solution.py:15
  42.4 10.4 %collective-permute-start.5 = (bf16[128,512]{1,0:T(8,128)(2,1)}, bf16[128,512]{1,0:T(8,128)(2,1)}, u32[]{:S(2)}, u32[]{:S(2)}) collective-permute-start(bf16[128,512]{1,0:T(8,128)(2,1)} %collective-permute-done.3), channel_id=1, source_target_pairs={{0,8},{8,16},{16,24},{24,32},{32,40},{40,48},{48,56},{56,64},{64,7... | collective-permute-start | bytes 393224 | tf_op jit(solution)/shard_map/ppermute | solution.py:15
  44.9 13.6 %collective-permute-start.6 = (bf16[128,512]{0,1:T(8,128)(2,1)}, bf16[128,512]{0,1:T(8,128)(2,1)}, u32[]{:S(2)}, u32[]{:S(2)}) collective-permute-start(bf16[128,512]{0,1:T(8,128)(2,1)} %collective-permute-done.4), channel_id=1, source_target_pairs={{0,8},{8,16},{16,24},{24,32},{32,40},{40,48},{48,56},{56,64},{64,7... | collective-permute-start | bytes 393224 | tf_op jit(solution)/shard_map/ppermute | solution.py:15
  53.8 6.4 %copy-start.6 = (f32[128,4,8]{0,2,1:T(8,128)S(1)}, f32[128,4,8]{0,2,1:T(8,128)}, u32[]{:S(2)}) copy-start(f32[128,4,8]{0,2,1:T(8,128)} %get-tuple-element.43) | copy-start | bytes 49156
  53.8 6.4 %copy-start.7 = (f32[128,4,8]{0,2,1:T(8,128)S(1)}, f32[128,4,8]{0,2,1:T(8,128)}, u32[]{:S(2)}) copy-start(f32[128,4,8]{0,2,1:T(8,128)} %get-tuple-element.39) | copy-start | bytes 49156
  53.9 6.4 %copy-start.8 = (f32[128,4,8]{0,2,1:T(8,128)S(1)}, f32[128,4,8]{0,2,1:T(8,128)}, u32[]{:S(2)}) copy-start(f32[128,4,8]{0,2,1:T(8,128)} %get-tuple-element.37) | copy-start | bytes 49156
  53.9 15.1 %collective-permute-start.7 = (bf16[128,512]{1,0:T(8,128)(2,1)}, bf16[128,512]{1,0:T(8,128)(2,1)}, u32[]{:S(2)}, u32[]{:S(2)}) collective-permute-start(bf16[128,512]{1,0:T(8,128)(2,1)} %collective-permute-done.5), channel_id=1, source_target_pairs={{0,8},{8,16},{16,24},{24,32},{32,40},{40,48},{48,56},{56,64},{64,7... | collective-permute-start | bytes 393224 | tf_op jit(solution)/shard_map/ppermute | solution.py:15
  58.5 2.2 %copy-start.1 = (f32[128,4,8,128]{0,3,2,1:T(8,128)S(1)}, f32[128,4,8,128]{0,3,2,1:T(8,128)}, u32[]{:S(2)}) copy-start(f32[128,4,8,128]{0,3,2,1:T(8,128)} %get-tuple-element.38) | copy-start | bytes 6291460
  60.2 1.3 %copy-start.2 = (f32[128,4,8,128]{0,3,2,1:T(8,128)}, f32[128,4,8,128]{0,3,2,1:T(8,128)S(1)}, u32[]{:S(2)}) copy-start(f32[128,4,8,128]{0,3,2,1:T(8,128)S(1)} %get-tuple-element.36) | copy-start | bytes 6291460
  60.3 8.7 %copy-start.4 = (f32[128,4,8]{0,2,1:T(8,128)}, f32[128,4,8]{0,2,1:T(8,128)S(1)}, u32[]{:S(2)}) copy-start(f32[128,4,8]{0,2,1:T(8,128)S(1)} %get-tuple-element.10) | copy-start | bytes 49156
  60.3 2.3 %copy-start = (f32[128,4,8,128]{0,3,2,1:T(8,128)S(1)}, f32[128,4,8,128]{0,3,2,1:T(8,128)}, u32[]{:S(2)}) copy-start(f32[128,4,8,128]{0,3,2,1:T(8,128)} %get-tuple-element.40) | copy-start | bytes 6291460
  62.6 0.7 copy-start.11
  63.4 1.8 %copy-start.10 = (f32[4,128]{1,0:T(4,128)S(1)}, f32[4,128]{1,0:T(4,128)}, u32[]{:S(2)}) copy-start(f32[4,128]{1,0:T(4,128)} %get-tuple-element.26) | copy-start | bytes 6148
  65.2 1.9 %copy-start.9 = (f32[4,128]{1,0:T(4,128)S(1)}, f32[4,128]{1,0:T(4,128)}, u32[]{:S(2)}) copy-start(f32[4,128]{1,0:T(4,128)} %get-tuple-element.28) | copy-start | bytes 6148
  67.0 1.9 %copy-start.5 = (f32[128,4,8]{0,2,1:T(8,128)S(1)}, f32[128,4,8]{0,2,1:T(8,128)}, u32[]{:S(2)}) copy-start(f32[128,4,8]{0,2,1:T(8,128)} %fusion.6) | copy-start | bytes 49156
  67.0 3.0 %copy-start.3 = (f32[128,4,8,128]{0,3,2,1:T(8,128)S(1)}, f32[128,4,8,128]{0,3,2,1:T(8,128)}, u32[]{:S(2)}) copy-start(f32[128,4,8,128]{0,3,2,1:T(8,128)} %copy-done.2) | copy-start | bytes 6291460
  67.0 3.0 %copy-start.13 = (f32[4,128]{1,0:T(4,128)S(1)}, f32[4,128]{1,0:T(4,128)}, u32[]{:S(2)}) copy-start(f32[4,128]{1,0:T(4,128)} %get-tuple-element.20) | copy-start | bytes 6148
where the time goes:
time: 76.7 us; the launch traced here: 76 us
  starting transfers between devices  33.2 us (43%)
  matrix products  22.4 us (29%)
  local copies, waits for them, and re-layouts  13.9 us (18%)
  other arithmetic  5.92 us (8%)
    ppermute x8, starting transfers between devices, shifted(): return lax.ppermute(block, axis, route)  33.2 us
    dot_general x5, matrix products, attend_tile(): jnp.einsum('tgjs,sgd->tgjd', weighted, vblock, preferred_element_type=jnp...  12.1 us
    dot_general x5, matrix products, attend_tile(): jnp.einsum('tgjd,sgd->tgjs', qview, kblock, preferred_element_type=jnp.fl...  10.3 us
    ppermute x4, local copies, waits for them, and re-layouts, shifted(): return lax.ppermute(block, axis, route)  4.08 us
    unnamed x30, local copies, waits for them, and re-layouts  4.07 us
    reduce_sum x5, other arithmetic, attend_tile(): total = total * factor + jnp.sum(prob, axis=-1)  2.47 us
    transpose x5, other arithmetic, attend_tile(): weighted = (prob * scales[:, 1, :].T[None, :, None, :]).astype(jnp.bfloat16)  2.39 us
  transfers between devices with their start and end apart: 8, of which 0 were waited for; matrix products, arithmetic and copies ran while one was open for 43% of the time, Pallas kernels for 0%

commit v1 on v0

v1 whole, which is shorter than its diff:
```python
import functools
import math

import jax
import jax.numpy as jnp
from jax import lax
from jax.experimental import pallas as pl
from jax.experimental.pallas import tpu as pltpu
from jax.sharding import PartitionSpec as P

SCALE_BLOCK = 32
HEAD = 128
ROW = 4
LOW = -1e30
CONTRACT_LAST = (((1,), (1,)), ((), ()))


def attend_kernel(docs, scales, *refs, backs, groups, rows):
    count = len(backs)
    queries, keys, values = refs[0], refs[1 : 1 + count], refs[1 + count : 1 + 2 * count]
    out, mask, kparts, vparts = refs[1 + 2 * count :]
    group = pl.program_id(0)
    first = lax.axis_index("ctx") * rows
    span = count * rows
    heads = queries.shape[1] // HEAD

    @pl.when(group == 0)
    def _():
        qpos = first + lax.broadcasted_iota(jnp.int32, (rows, HEAD), 0)

        def visit(doc, carry):
            end, start = carry
            end = end + docs[doc]
            return end, jnp.where(end <= qpos, end, start)

        _, start = lax.fori_loop(0, docs.shape[0], visit, (0, jnp.zeros((rows, HEAD), jnp.int32)), unroll=8)
        for slot, back in enumerate(backs):
            kpos = first - back * rows + lax.broadcasted_iota(jnp.int32, (rows, rows), 1)
            keep = kpos >= start[:, :1]
            if back == 0:
                keep = keep & (kpos <= qpos[:, :1])
            mask[:, slot * rows : (slot + 1) * rows] = jnp.where(keep, 0.0, LOW)

    lane = lax.broadcasted_iota(jnp.int32, (SCALE_BLOCK, HEAD), 1)
    wide = lax.broadcasted_iota(jnp.int32, (1, rows), 1)
    level = []
    for slot, back in enumerate(backs):
        line = jnp.zeros((1, rows), jnp.float32)
        for piece in range(rows // SCALE_BLOCK):
            block = jnp.maximum(first // SCALE_BLOCK - back * (rows // SCALE_BLOCK) + piece, 0)
            kscale = scales[block * 2 * groups + group] * (math.log2(math.e) / math.sqrt(HEAD))
            vscale = scales[block * 2 * groups + groups + group]
            source = pl.ds(piece * SCALE_BLOCK, SCALE_BLOCK)
            target = pl.ds(slot * rows + piece * SCALE_BLOCK, SCALE_BLOCK)
            scaled = keys[slot][source, :].astype(jnp.float32) * kscale
            high = scaled.astype(jnp.bfloat16)
            kparts[target, :HEAD] = high
            kparts[target, HEAD:] = (scaled - high.astype(jnp.float32)).astype(jnp.bfloat16)
            inverse = 1.0 / jnp.full((SCALE_BLOCK, HEAD), vscale, jnp.float32)
            high = inverse.astype(jnp.bfloat16).astype(jnp.float32)
            ones = jnp.where(lane == 0, high, jnp.where(lane == 1, inverse - high, 0.0))
            vparts[target, :HEAD] = values[slot][source, :]
            vparts[target, HEAD:] = ones.astype(jnp.bfloat16)
            line = jnp.where(wide // SCALE_BLOCK == piece, vscale, line)
        level.append(jnp.log2(line))
    bias = mask[...] + jnp.concatenate(level, axis=1)

    query = jnp.concatenate([queries[:, h * HEAD : (h + 1) * HEAD] for h in range(heads)], axis=0)
    query = jnp.concatenate([query, query], axis=1)
    score = lax.dot_general(query, kparts[...], CONTRACT_LAST, preferred_element_type=jnp.float32)
    score = score.reshape(heads, rows, span) + bias[None]
    top = jnp.max(score, axis=-1, keepdims=True)
    weighted = jnp.exp2(score - top).astype(jnp.bfloat16).reshape(heads * rows, span)
    both = jnp.dot(weighted, vparts[...], preferred_element_type=jnp.float32)
    total = both[:, HEAD : HEAD + 1] + both[:, HEAD + 1 : HEAD + 2]
    result = (both[:, :HEAD] / total).astype(jnp.bfloat16)
    for h in range(heads):
        out[:, h * HEAD : (h + 1) * HEAD] = result[h * rows : (h + 1) * rows]


def attend(docs, scales, queries, blocks, backs):
    rows, width = queries.shape
    groups = blocks[0].shape[1] // (2 * HEAD)
    count = len(backs)
    span = count * rows
    per = width // groups
    smem = pl.BlockSpec(memory_space=pltpu.SMEM)
    return pl.pallas_call(
        functools.partial(attend_kernel, backs=backs, groups=groups, rows=rows),
        grid=(groups,),
        in_specs=[smem, smem, pl.BlockSpec((rows, per), lambda g: (0, g))]
        + [pl.BlockSpec((rows, HEAD), lambda g: (0, g))] * count
        + [pl.BlockSpec((rows, HEAD), lambda g: (0, groups + g))] * count,
        out_specs=pl.BlockSpec((rows, per), lambda g: (0, g)),
        out_shape=jax.ShapeDtypeStruct((rows, width), jnp.bfloat16),
        scratch_shapes=[
            pltpu.VMEM((rows, span), jnp.float32),
            pltpu.VMEM((span, 2 * HEAD), jnp.bfloat16),
            pltpu.VMEM((span, 2 * HEAD), jnp.bfloat16),
        ],
        compiler_params=pltpu.CompilerParams(vmem_limit_bytes=48 * 2**20),
    )(docs, scales, queries, *blocks, *blocks)


def ahead(block, distance):
    size = lax.axis_size("ctx")
    return lax.ppermute(block, "ctx", [(i, i + distance) for i in range(size - distance)])


def in_row(block, step):
    size = lax.axis_size("ctx")
    return lax.ppermute(block, "ctx", [(i, i // ROW * ROW + (i + step) % ROW) for i in range(size)])


def per_device(queries, keys, values, key_value_scales, doc_lengths):
    own = jnp.concatenate([keys, values], axis=1)
    column = lax.axis_index("ctx") % ROW
    fourth = ahead(own, 4)
    second = ahead(own, 2)
    third = in_row(jnp.where(column == 0, own, fourth), ROW - 1)
    nearest = in_row(jnp.where(column < ROW - 1, own, fourth), 1)
    scales = key_value_scales.reshape(-1)
    blocks = (own, fourth, second, third, nearest)
    return attend(doc_lengths, scales, queries, blocks, (0, 4, 2, 3, 1))


def solution(mesh):
    return jax.shard_map(
        per_device,
        mesh=mesh,
        in_specs=(
            P(("seq", "ctx"), None),
            P(("seq", "ctx"), None),
            P(("seq", "ctx"), None),
            P("seq", None, None),
            P("seq"),
        ),
        out_specs=P(("seq", "ctx"), None),
        check_vma=False,
    )
```

time: 76.7 us -> 37.6 us (0.49)
  the two profiles are of different devices: /device:TPU:238 before, /device:TPU:273 now
where the time goes in v1:
time: 37.6 us; the launch traced here: 37.4 us
  starting transfers between devices  14.4 us (38%)
  waiting for transfers between devices  10.9 us (29%)
  Pallas kernels  10.4 us (28%)
  local copies, waits for them, and re-layouts  1.55 us (4%)
    pallas_call x1, Pallas kernels, attend(): pl.pallas_call(functools.partial(attend_kernel, backs=backs, groups=group...  10.4 us
    ppermute x2, starting transfers between devices, ahead(): lax.ppermute(block, 'ctx', [(i, i + distance) for i in range(size - dista...  7.86 us
    ppermute x2, waiting for transfers between devices, in_row(): lax.ppermute(block, 'ctx', [(i, i // ROW * ROW + (i + step) % ROW) for i...  6.62 us
    ppermute x2, starting transfers between devices, in_row(): lax.ppermute(block, 'ctx', [(i, i // ROW * ROW + (i + step) % ROW) for i...  6.49 us
    ppermute x2, waiting for transfers between devices, ahead(): lax.ppermute(block, 'ctx', [(i, i + distance) for i in range(size - dista...  4.27 us
    unnamed x10, local copies, waits for them, and re-layouts  1.2 us
  transfers between devices with their start and end apart: 4, of which 3 were waited for; matrix products, arithmetic and copies ran while one was open for 1% of the time, Pallas kernels for 0%

profile of v1, /device:TPU:273, one launch (start us, length us, event | category | flops | bytes accessed | tf_op | source)
XLA Modules:
  0.0 37.4 jit_solution(602701158691797513)
XLA Ops:
  0.0 0.0 copy-start.2
  0.0 0.0 copy-start
  0.0 1.0 %constant_dynamic-update-slice_fusion.1 = bf16[128,1024]{1,0:T(8,128)(2,1)S(1)} fusion(bf16[128,512]{1,0:T(8,128)(2,1)} %param.6), kind=kLoop, calls=%fused_computation.3 | loop fusion | bytes 262144
  1.0 0.0 copy-done.2
  1.0 3.2 %collective-permute-start = (bf16[128,1024]{1,0:T(8,128)(2,1)S(1)}, bf16[128,1024]{1,0:T(8,128)(2,1)S(1)}, u32[]{:S(2)}, u32[]{:S(2)}) collective-permute-start(bf16[128,1024]{1,0:T(8,128)(2,1)S(1)} %constant_dynamic-update-slice_fusion.refs_1_.refs_6_), channel_id=1, source_target_pairs={{0,32},{8,40},{16,48},{24,56},{32,64},{40,72},{48,80},{56,88},{64,... | collective-permute-start | bytes 786440 | tf_op jit(solution)/shard_map/ppermute | solution.py:107
  4.3 4.7 %collective-permute-start.1 = (bf16[128,1024]{1,0:T(8,128)(2,1)S(1)}, bf16[128,1024]{1,0:T(8,128)(2,1)S(1)}, u32[]{:S(2)}, u32[]{:S(2)}) collective-permute-start(bf16[128,1024]{1,0:T(8,128)(2,1)S(1)} %constant_dynamic-update-slice_fusion.refs_1_.refs_6_), channel_id=1, source_target_pairs={{0,16},{8,24},{16,32},{24,40},{32,48},{40,56},{48,64},{56,72},{64,... | collective-permute-start | bytes 786440 | tf_op jit(solution)/shard_map/ppermute | solution.py:107
  8.9 3.3 %collective-permute-done.refs_2_.refs_7_ = bf16[128,1024]{1,0:T(8,128)(2,1)S(1)} collective-permute-done((bf16[128,1024]{1,0:T(8,128)(2,1)S(1)}, bf16[128,1024]{1,0:T(8,128)(2,1)S(1)}, u32[]{:S(2)}, u32[]{:S(2)}) %collective-permute-start) | collective-permute-done | bytes 262176 | tf_op jit(solution)/shard_map/ppermute | solution.py:107
  12.2 0.0 copy-start.3
  12.3 3.1 %collective-permute-start.3 = (bf16[128,1024]{1,0:T(8,128)(2,1)S(1)}, bf16[128,1024]{1,0:T(8,128)(2,1)S(1)}, u32[]{:S(2)}, u32[]{:S(2)}) collective-permute-start(bf16[128,1024]{1,0:T(8,128)(2,1)S(1)} %get-tuple-element.5), channel_id=1, source_target_pairs={{0,8},{8,16},{16,24},{24,0},{32,40},{40,48},{48,56},{56,32},{64,72... | collective-permute-start | bytes 786440 | tf_op jit(solution)/shard_map/ppermute | solution.py:112
  15.4 3.4 %collective-permute-start.2 = (bf16[128,1024]{1,0:T(8,128)(2,1)S(1)}, bf16[128,1024]{1,0:T(8,128)(2,1)S(1)}, u32[]{:S(2)}, u32[]{:S(2)}) collective-permute-start(bf16[128,1024]{1,0:T(8,128)(2,1)S(1)} %get-tuple-element.6), channel_id=1, source_target_pairs={{0,24},{8,0},{16,8},{24,16},{32,56},{40,32},{48,40},{56,48},{64,88... | collective-permute-start | bytes 786440 | tf_op jit(solution)/shard_map/ppermute | solution.py:112
  18.8 0.0 copy-done.3
  18.8 0.2 copy.6
  19.0 0.0 copy-start.1
  19.0 0.3 reshape.3.scales
  19.3 1.0 %collective-permute-done.1.refs_3_.refs_8_ = bf16[128,1024]{1,0:T(8,128)(2,1)S(1)} collective-permute-done((bf16[128,1024]{1,0:T(8,128)(2,1)S(1)}, bf16[128,1024]{1,0:T(8,128)(2,1)S(1)}, u32[]{:S(2)}, u32[]{:S(2)}) %collective-permute-start.1) | collective-permute-done | bytes 262176 | tf_op jit(solution)/shard_map/ppermute | solution.py:107
  20.3 6.6 %collective-permute-done.3.refs_5_.refs_10_ = bf16[128,1024]{1,0:T(8,128)(2,1)S(1)} collective-permute-done((bf16[128,1024]{1,0:T(8,128)(2,1)S(1)}, bf16[128,1024]{1,0:T(8,128)(2,1)S(1)}, u32[]{:S(2)}, u32[]{:S(2)}) %collective-permute-start.3) | collective-permute-done | bytes 262176 | tf_op jit(solution)/shard_map/ppermute | solution.py:112
  26.9 0.0 collective-permute-done.2.refs_4_.refs_9_
  26.9 0.0 copy-done
  26.9 0.0 copy-done.1
  26.9 10.4 %shard_map.55 = bf16[128,4096]{1,0:T(8,128)(2,1)} custom-call(s32[32]{0:T(128)S(1)} %copy-done.1, f32[2048]{0:T(1024)S(1)} %reshape.3.scales, bf16[128,4096]{1,0:T(8,128)(2,1)S(1)} %copy-done, bf16[128,1024]{1,0:T(8,128)(2,1)S(1)} %constant_dynamic-update-slice_fusion.refs_1_.refs_6_, bf16[128,1024]{1,0:T(8,128)(2,1)S(1)} %collective-permute-done.refs_2_.refs_7_, ...), custom_call_target="tpu_custom_call" | custom-call | tf_op jit(solution)/shard_map/pallas_call | solution.py:88
  (2 shorter events, 0.1 us)
Async XLA Ops:
  0.0 1.0 %copy-start.2 = (bf16[128,512]{1,0:T(8,128)(2,1)S(1)}, bf16[128,512]{1,0:T(8,128)(2,1)}, u32[]{:S(2)}) copy-start(bf16[128,512]{1,0:T(8,128)(2,1)} %param.7) | copy-start | bytes 393220
  0.0 26.9 %copy-start = (bf16[128,4096]{1,0:T(8,128)(2,1)S(1)}, bf16[128,4096]{1,0:T(8,128)(2,1)}, u32[]{:S(2)}) copy-start(bf16[128,4096]{1,0:T(8,128)(2,1)} %refs_0_.1) | copy-start | bytes 3145732
  1.0 11.2 %collective-permute-start = (bf16[128,1024]{1,0:T(8,128)(2,1)S(1)}, bf16[128,1024]{1,0:T(8,128)(2,1)S(1)}, u32[]{:S(2)}, u32[]{:S(2)}) collective-permute-start(bf16[128,1024]{1,0:T(8,128)(2,1)S(1)} %constant_dynamic-update-slice_fusion.refs_1_.refs_6_), channel_id=1, source_target_pairs={{0,32},{8,40},{16,48},{24,56},{32,64},{40,72},{48,80},{56,88},{64,... | collective-permute-start | bytes 786440 | tf_op jit(solution)/shard_map/ppermute | solution.py:107
  4.3 16.0 %collective-permute-start.1 = (bf16[128,1024]{1,0:T(8,128)(2,1)S(1)}, bf16[128,1024]{1,0:T(8,128)(2,1)S(1)}, u32[]{:S(2)}, u32[]{:S(2)}) collective-permute-start(bf16[128,1024]{1,0:T(8,128)(2,1)S(1)} %constant_dynamic-update-slice_fusion.refs_1_.refs_6_), channel_id=1, source_target_pairs={{0,16},{8,24},{16,32},{24,40},{32,48},{40,56},{48,64},{56,72},{64,... | collective-permute-start | bytes 786440 | tf_op jit(solution)/shard_map/ppermute | solution.py:107
  12.2 6.6 %copy-start.3 = (f32[256,2,4]{0,2,1:T(4,128)S(1)}, f32[256,2,4]{0,2,1:T(4,128)}, u32[]{:S(2)}) copy-start(f32[256,2,4]{0,2,1:T(4,128)} %param.8) | copy-start | bytes 24580
  12.3 14.6 %collective-permute-start.3 = (bf16[128,1024]{1,0:T(8,128)(2,1)S(1)}, bf16[128,1024]{1,0:T(8,128)(2,1)S(1)}, u32[]{:S(2)}, u32[]{:S(2)}) collective-permute-start(bf16[128,1024]{1,0:T(8,128)(2,1)S(1)} %get-tuple-element.5), channel_id=1, source_target_pairs={{0,8},{8,16},{16,24},{24,0},{32,40},{40,48},{48,56},{56,32},{64,72... | collective-permute-start | bytes 786440 | tf_op jit(solution)/shard_map/ppermute | solution.py:112
  15.4 11.5 %collective-permute-start.2 = (bf16[128,1024]{1,0:T(8,128)(2,1)S(1)}, bf16[128,1024]{1,0:T(8,128)(2,1)S(1)}, u32[]{:S(2)}, u32[]{:S(2)}) collective-permute-start(bf16[128,1024]{1,0:T(8,128)(2,1)S(1)} %get-tuple-element.6), channel_id=1, source_target_pairs={{0,24},{8,0},{16,8},{24,16},{32,56},{40,32},{48,40},{56,48},{64,88... | collective-permute-start | bytes 786440 | tf_op jit(solution)/shard_map/ppermute | solution.py:112
  19.0 8.0 %copy-start.1 = (s32[32]{0:T(128)S(1)}, s32[32]{0:T(128)}, u32[]{:S(2)}) copy-start(s32[32]{0:T(128)} %docs.1) | copy-start | bytes 388

commit v2 on v0

v2 whole, which is shorter than its diff:
```python
import functools
import math

import jax
import jax.numpy as jnp
from jax import lax
from jax.experimental import pallas as pl
from jax.experimental.pallas import tpu as pltpu
from jax.sharding import PartitionSpec as P

SCALE_BLOCK = 32
HEAD = 128
LOW = -1e30
LAST = (((1,), (1,)), ((), ()))
EXTRA = 16
CHUNK = 8
ROW = 4


def table_kernel(docs, scales, table, *, groups, rows, backs):
    first = lax.axis_index("ctx") * rows
    pieces = rows // SCALE_BLOCK
    qpos = first + lax.broadcasted_iota(jnp.int32, (8, rows), 1)

    def visit(doc, carry):
        end, start = carry
        end = end + docs[doc]
        return end, jnp.where(end <= qpos, end, start)

    _, start = lax.fori_loop(0, docs.shape[0], visit, (0, jnp.zeros((8, rows), jnp.int32)), unroll=8)
    lane = lax.broadcasted_iota(jnp.int32, (1, rows), 1) // SCALE_BLOCK
    for slot, back in enumerate(backs):
        kpos = first - back * rows + lax.broadcasted_iota(jnp.int32, (rows, rows), 0)
        keep = kpos >= start[:1]
        if back == 0:
            keep = keep & (kpos <= qpos[:1])
        table[slot, :rows, :] = jnp.where(keep, 0.0, LOW)
        for group in range(groups):
            line = jnp.ones((1, rows), jnp.float32)
            for piece in range(pieces):
                block = jnp.maximum(first // SCALE_BLOCK - back * pieces + piece, 0)
                kscale = scales[block * 2 * groups + group] * (math.log2(math.e) / math.sqrt(HEAD))
                vscale = scales[block * 2 * groups + groups + group]
                at = rows + group * (2 * pieces + 1) + 2 * piece
                table[slot, at : at + 1, :] = jnp.full((1, rows), kscale, jnp.float32)
                table[slot, at + 1 : at + 2, :] = jnp.log2(jnp.full((1, rows), vscale, jnp.float32))
                line = jnp.where(lane == piece, vscale, line)
            at = rows + group * (2 * pieces + 1) + 2 * pieces
            table[slot, at : at + 1, :] = 1.0 / line


def make_table(docs, scales, rows, groups, backs):
    depth = rows + groups * (2 * (rows // SCALE_BLOCK) + 1)
    depth = (depth + 7) // 8 * 8
    smem = pl.BlockSpec(memory_space=pltpu.SMEM)
    return pl.pallas_call(
        functools.partial(table_kernel, groups=groups, rows=rows, backs=backs),
        in_specs=[smem, smem],
        out_specs=pl.BlockSpec(memory_space=pltpu.VMEM),
        out_shape=jax.ShapeDtypeStruct((len(backs), depth, rows), jnp.float32),
    )(docs, scales)


def kernel(*refs, slots, groups, rows, state, final, chunk):
    count = len(slots)
    refs = list(refs)
    sources = refs[: 2 + count + 2 * state]
    refs = refs[len(sources) :]
    if final:
        out = refs[0]
        refs = refs[1:]
    else:
        acc_out, stat_out = refs[:2]
        refs = refs[2:]
    buffers = sources
    bias, kparts, vparts, scores, probs = refs[:5]
    if final:
        stage, out_sems = refs[5:]
    width = sources[1].shape[1]
    heads = width // HEAD
    per = heads // groups
    pieces = rows // SCALE_BLOCK

    table, queries, blocks = buffers[0], buffers[1], buffers[2 : 2 + count]
    if state:
        acc_in, stat_in = buffers[2 + count], buffers[3 + count]

    deep = lax.broadcasted_iota(jnp.int32, (EXTRA, rows), 0)

    def prepare(group):
        at = group % 3
        for slot in range(count):
            base = rows + group * (2 * pieces + 1)
            for piece in range(pieces):
                source = pl.ds(piece * SCALE_BLOCK, SCALE_BLOCK)
                target = pl.ds(slot * rows + piece * SCALE_BLOCK, SCALE_BLOCK)
                kscale = table[slots[slot], base + 2 * piece : base + 2 * piece + 1, :]
                scaled = blocks[slot][source, group * HEAD : (group + 1) * HEAD].astype(jnp.float32) * kscale
                high = scaled.astype(jnp.bfloat16)
                kparts[at, target, :HEAD] = high
                kparts[at, target, HEAD:] = (scaled - high.astype(jnp.float32)).astype(jnp.bfloat16)
                bias[at, target, :] = table[slots[slot], source, :] + table[slots[slot], base + 2 * piece + 1 : base + 2 * piece + 2, :]
            inverse = table[slots[slot], base + 2 * pieces : base + 2 * pieces + 1, :]
            high = inverse.astype(jnp.bfloat16).astype(jnp.float32)
            ones = jnp.where(deep == 0, high, jnp.where(deep == 1, inverse - high, 0.0))
            columns = pl.ds(slot * rows, rows)
            vparts[at, :HEAD, columns] = blocks[slot][:, (groups + group) * HEAD : (groups + group + 1) * HEAD].T
            vparts[at, HEAD:, columns] = ones.astype(jnp.bfloat16)

    steps = heads // chunk
    tops = {}

    def some(step):
        return range(step * chunk, (step + 1) * chunk)

    def across(ref, offset, step):
        return jnp.concatenate([ref[offset + h : offset + h + 1, :] for h in some(step)], axis=1)

    def score_part(step):
        group = step * chunk // per
        if step * chunk % per == 0:
            prepare(group)
        query = jnp.concatenate([queries[:, h * HEAD : (h + 1) * HEAD] for h in some(step)], axis=0)
        query = jnp.concatenate([query, query], axis=1)
        score = lax.dot_general(kparts[group % 3], query, LAST, preferred_element_type=jnp.float32)
        score = score + jnp.concatenate([bias[group % 3]] * chunk, axis=1)
        scores[step % 2] = score
        top = jnp.max(score, axis=0, keepdims=True)
        if state:
            top = jnp.maximum(top, across(stat_in, 0, step))
        tops[step] = top

    def prob_part(step):
        probs[step % 2] = jnp.exp2(scores[step % 2] - tops[step]).astype(jnp.bfloat16)

    def send(group):
        columns = pl.ds(group * per * HEAD, per * HEAD)
        return pltpu.make_async_copy(stage.at[:, columns], out.at[:, columns], out_sems.at[group])

    def value_part(step):
        group = step * chunk // per
        both = jnp.dot(vparts[group % 3], probs[step % 2], preferred_element_type=jnp.float32)
        total = both[HEAD : HEAD + 1] + both[HEAD + 1 : HEAD + 2]
        result = both[:HEAD]
        if state:
            keep = jnp.exp2(across(stat_in, 0, step) - tops[step])
            total = total + keep * across(stat_in, heads, step)
            old = jnp.concatenate([acc_in[h * HEAD : (h + 1) * HEAD, :] for h in some(step)], axis=1)
            result = result + keep * old
        if final:
            result = result * (1.0 / total)
        for at, h in enumerate(some(step)):
            lanes = slice(at * rows, (at + 1) * rows)
            if final:
                stage[:, h * HEAD : (h + 1) * HEAD] = result[:, lanes].T.astype(jnp.bfloat16)
            else:
                acc_out[h * HEAD : (h + 1) * HEAD, :] = result[:, lanes]
                stat_out[h : h + 1, :] = tops[step][:, lanes]
                stat_out[heads + h : heads + h + 1, :] = total[:, lanes]
        if final and (step + 1) * chunk % per == 0:
            send(group).start()

    for step in range(steps + 2):
        if step < steps:
            score_part(step)
        if 1 <= step <= steps:
            prob_part(step - 1)
        if 2 <= step:
            value_part(step - 2)
    if final:
        for group in range(groups):
            send(group).wait()


def attend(table, queries, blocks, slots, state=None, final=True, chunk=CHUNK):
    rows, width = queries.shape
    groups = blocks[0].shape[1] // (2 * HEAD)
    count = len(slots)
    span = count * rows
    heads = width // HEAD
    anywhere = pl.BlockSpec(memory_space=pl.ANY)
    state_shapes = [
        jax.ShapeDtypeStruct((width, rows), jnp.float32),
        jax.ShapeDtypeStruct((2 * heads, rows), jnp.float32),
    ]
    held = state is not None
    scratch = []
    scratch += [
        pltpu.VMEM((3, span, rows), jnp.float32),
        pltpu.VMEM((3, span, 2 * HEAD), jnp.bfloat16),
        pltpu.VMEM((3, HEAD + EXTRA, span), jnp.bfloat16),
        pltpu.VMEM((2, span, chunk * rows), jnp.float32),
        pltpu.VMEM((2, span, chunk * rows), jnp.bfloat16),
    ]
    if final:
        scratch += [pltpu.VMEM((rows, width), jnp.bfloat16), pltpu.SemaphoreType.DMA((groups,))]
    return pl.pallas_call(
        functools.partial(kernel, slots=slots, groups=groups, rows=rows, state=held, final=final, chunk=chunk),
        in_specs=[pl.BlockSpec(memory_space=pltpu.VMEM)] * (2 + count + 2 * held),
        out_specs=anywhere if final else [pl.BlockSpec(memory_space=pltpu.VMEM)] * 2,
        out_shape=jax.ShapeDtypeStruct((rows, width), jnp.bfloat16) if final else state_shapes,
        scratch_shapes=scratch,
        compiler_params=pltpu.CompilerParams(vmem_limit_bytes=40 * 2**20),
        cost_estimate=pl.CostEstimate(
            flops=4 * rows * width * span, bytes_accessed=4 * rows * width, transcendentals=heads * rows * span
        ),
    )(table, queries, *blocks, *(state if held else ()))


def ahead(block, distance):
    size = lax.axis_size("ctx")
    return lax.ppermute(block, "ctx", [(i, i + distance) for i in range(size - distance)])


def in_row(block, step):
    size = lax.axis_size("ctx")
    return lax.ppermute(block, "ctx", [(i, i // ROW * ROW + (i + step) % ROW) for i in range(size)])


def per_device(queries, keys, values, key_value_scales, doc_lengths):
    rows = queries.shape[0]
    groups = key_value_scales.shape[2]
    own = jnp.concatenate([keys, values], axis=1)
    column = lax.axis_index("ctx") % ROW
    fourth = ahead(own, 4)
    second = ahead(own, 2)
    third = in_row(jnp.where(column == 0, own, fourth), ROW - 1)
    nearest = in_row(jnp.where(column < ROW - 1, own, fourth), 1)
    table = make_table(doc_lengths, key_value_scales.reshape(-1), rows, groups, (0, 4, 2, 3, 1))
    state = attend(table, queries, (own, fourth, second), (0, 1, 2), final=False)
    state = attend(table, queries, (third,), (3,), state=state, final=False)
    return attend(table, queries, (nearest,), (4,), state=state)


def solution(mesh):
    return jax.shard_map(
        per_device,
        mesh=mesh,
        in_specs=(
            P(("seq", "ctx"), None),
            P(("seq", "ctx"), None),
            P(("seq", "ctx"), None),
            P("seq", None, None),
            P("seq"),
        ),
        out_specs=P(("seq", "ctx"), None),
        check_vma=False,
    )
```

time: 76.7 us -> 33.1 us (0.43)
  the two profiles are of different devices: /device:TPU:238 before, /device:TPU:294 now
where the time goes in v2:
time: 33.1 us; the launch traced here: 32.7 us
  starting transfers between devices  14.6 us (44%)
  Pallas kernels  7.65 us (23%)
  waiting for transfers between devices  5.58 us (17%)
  local copies, waits for them, and re-layouts  4.73 us (14%)
    ppermute x2, starting transfers between devices, ahead(): lax.ppermute(block, 'ctx', [(i, i + distance) for i in range(size - dista...  7.59 us
    ppermute x2, starting transfers between devices, in_row(): lax.ppermute(block, 'ctx', [(i, i // ROW * ROW + (i + step) % ROW) for i...  7.05 us
    pallas_call x3, Pallas kernels, attend(): pl.pallas_call(functools.partial(kernel, slots=slots, groups=groups, rows...  5.9 us
    ppermute x2, waiting for transfers between devices, ahead(): lax.ppermute(block, 'ctx', [(i, i + distance) for i in range(size - dista...  5.57 us
    unnamed x6, local copies, waits for them, and re-layouts  2.88 us
    pallas_call x1, Pallas kernels, make_table(): pl.pallas_call(functools.partial(table_kernel, groups=groups, rows=rows,...  1.75 us
    reshape x1, local copies, waits for them, and re-layouts, per_device(): key_value_scales.reshape(-1)  0.93 us
    concatenate x1, local copies, waits for them, and re-layouts, per_device(): own = jnp.concatenate([keys, values], axis=1)  0.92 us
  transfers between devices with their start and end apart: 4, of which 1 were waited for; matrix products, arithmetic and copies ran while one was open for 6% of the time, Pallas kernels for 16%

profile of v2, /device:TPU:294, one launch (start us, length us, event | category | flops | bytes accessed | tf_op | source)
XLA Modules:
  0.0 32.7 jit_solution(18271084800718329016)
XLA Ops:
  0.0 0.0 copy-start
  0.0 1.0 %constant_dynamic-update-slice_fusion.1 = bf16[128,1024]{1,0:T(8,128)(2,1)S(1)} fusion(bf16[128,512]{1,0:T(8,128)(2,1)} %param.6), kind=kLoop, calls=%fused_computation.3 | loop fusion | bytes 262144
  1.0 0.9 %constant_dynamic-update-slice_fusion.refs_2_ = bf16[128,1024]{1,0:T(8,128)(2,1)S(1)} fusion(bf16[128,1024]{1,0:T(8,128)(2,1)S(1)} %constant_dynamic-update-slice_fusion.1, bf16[128,512]{1,0:T(8,128)(2,1)} %param.7), kind=kLoop, calls=%fused_computation.2 | loop fusion | bytes 262144 | tf_op jit(solution)/shard_map/concatenate | solution.py:223
  1.9 2.6 %collective-permute-start = (bf16[128,1024]{1,0:T(8,128)(2,1)S(1)}, bf16[128,1024]{1,0:T(8,128)(2,1)S(1)}, u32[]{:S(2)}, u32[]{:S(2)}) collective-permute-start(bf16[128,1024]{1,0:T(8,128)(2,1)S(1)} %constant_dynamic-update-slice_fusion.refs_2_), channel_id=1, source_target_pairs={{0,32},{8,40},{16,48},{24,56},{32,64},{40,72},{48,80},{56,88},{64,... | collective-permute-start | bytes 786440 | tf_op jit(solution)/shard_map/ppermute | solution.py:212
  4.5 5.0 %collective-permute-start.3 = (bf16[128,1024]{1,0:T(8,128)(2,1)S(1)}, bf16[128,1024]{1,0:T(8,128)(2,1)S(1)}, u32[]{:S(2)}, u32[]{:S(2)}) collective-permute-start(bf16[128,1024]{1,0:T(8,128)(2,1)S(1)} %constant_dynamic-update-slice_fusion.refs_2_), channel_id=1, source_target_pairs={{0,16},{8,24},{16,32},{24,40},{32,48},{40,56},{48,64},{56,72},{64,... | collective-permute-start | bytes 786440 | tf_op jit(solution)/shard_map/ppermute | solution.py:212
  9.6 5.6 %collective-permute-done.refs_3_ = bf16[128,1024]{1,0:T(8,128)(2,1)S(1)} collective-permute-done((bf16[128,1024]{1,0:T(8,128)(2,1)S(1)}, bf16[128,1024]{1,0:T(8,128)(2,1)S(1)}, u32[]{:S(2)}, u32[]{:S(2)}) %collective-permute-start) | collective-permute-done | bytes 262176 | tf_op jit(solution)/shard_map/ppermute | solution.py:212
  15.2 2.7 %collective-permute-start.2 = (bf16[128,1024]{1,0:T(8,128)(2,1)S(1)}, bf16[128,1024]{1,0:T(8,128)(2,1)S(1)}, u32[]{:S(2)}, u32[]{:S(2)}) collective-permute-start(bf16[128,1024]{1,0:T(8,128)(2,1)S(1)} %get-tuple-element.13), channel_id=1, source_target_pairs={{0,24},{8,0},{16,8},{24,16},{32,56},{40,32},{48,40},{56,48},{64,88... | collective-permute-start | bytes 786440 | tf_op jit(solution)/shard_map/ppermute | solution.py:217
  17.9 4.3 %collective-permute-start.1 = (bf16[128,1024]{1,0:T(8,128)(2,1)S(1)}, bf16[128,1024]{1,0:T(8,128)(2,1)S(1)}, u32[]{:S(2)}, u32[]{:S(2)}) collective-permute-start(bf16[128,1024]{1,0:T(8,128)(2,1)S(1)} %get-tuple-element.14), channel_id=1, source_target_pairs={{0,8},{8,16},{16,24},{24,0},{32,40},{40,48},{48,56},{56,32},{64,72... | collective-permute-start | bytes 786440 | tf_op jit(solution)/shard_map/ppermute | solution.py:217
  22.2 0.9 %copy.6 = f32[256,2,4]{2,1,0:T(2,128)S(1)} copy(f32[256,2,4]{0,2,1:T(4,128)} %param.8) | data formatting | bytes 16384 | tf_op args[3]
  23.1 0.9 %reshape.3.scales = f32[2048]{0:T(1024)} reshape(f32[256,2,4]{2,1,0:T(2,128)S(1)} %copy.6) | data formatting | bytes 16384 | tf_op jit(solution)/shard_map/reshape | solution.py:229
  24.0 1.8 %shard_map.55.refs_0_ = f32[5,168,128]{2,1,0:T(8,128)} custom-call(s32[32]{0:T(128)} %docs.1, f32[2048]{0:T(1024)} %reshape.3.scales), custom_call_target="tpu_custom_call" | custom-call | tf_op jit(solution)/shard_map/pallas_call | solution.py:56
  25.8 0.0 collective-permute-done.3.refs_4_
  25.8 0.0 copy-done
  25.8 0.0 copy-start.1
  25.8 1.0 %copy-done.1 = f32[5,168,128]{2,1,0:T(8,128)S(1)} copy-done((f32[5,168,128]{2,1,0:T(8,128)S(1)}, f32[5,168,128]{2,1,0:T(8,128)}, u32[]{:S(2)}) %copy-start.1) | copy-done | bytes 430104
  26.8 2.3 %shard_map.56 = (f32[4096,128]{1,0:T(8,128)S(1)}, f32[64,128]{1,0:T(8,128)S(1)}) custom-call(f32[5,168,128]{2,1,0:T(8,128)S(1)} %copy-done.1, bf16[128,4096]{1,0:T(8,128)(2,1)S(1)} %copy-done, bf16[128,1024]{1,0:T(8,128)(2,1)S(1)} %constant_dynamic-update-slice_fusion.refs_2_, bf16[128,1024]{1,0:T(8,128)(2,1)S(1)} %collective-permute-done.refs_3_, ...), custom_call_target="tpu_custom_call" | custom-call | flops 805306368 | bytes 2097152 | tf_op jit(solution)/shard_map/pallas_call | solution.py:197
  29.2 0.0 collective-permute-done.2.refs_2_
  29.2 1.3 %shard_map.57 = (f32[4096,128]{1,0:T(8,128)S(1)}, f32[64,128]{1,0:T(8,128)S(1)}) custom-call(f32[5,168,128]{2,1,0:T(8,128)S(1)} %copy-done.1, bf16[128,4096]{1,0:T(8,128)(2,1)S(1)} %copy-done, bf16[128,1024]{1,0:T(8,128)(2,1)S(1)} %collective-permute-done.2.refs_2_, f32[4096,128]{1,0:T(8,128)S(1)} %get-tuple-element.9.refs_3_, ...), custom_call_target="tpu_custom_call" | custom-call | flops 268435456 | bytes 2097152 | tf_op jit(solution)/shard_map/pallas_call | solution.py:197
  30.4 0.0 collective-permute-done.1.refs_2_
  30.4 2.3 %shard_map.58 = bf16[128,4096]{1,0:T(8,128)(2,1)} custom-call(f32[5,168,128]{2,1,0:T(8,128)S(1)} %copy-done.1, bf16[128,4096]{1,0:T(8,128)(2,1)S(1)} %copy-done, bf16[128,1024]{1,0:T(8,128)(2,1)S(1)} %collective-permute-done.1.refs_2_, f32[4096,128]{1,0:T(8,128)S(1)} %get-tuple-element.11.refs_3_, f32[64,128]{1,0:T(8,128)S(1)} %get-tuple-element.12.refs_4_), custom_call_target="tpu_custom_call" | custom-call | flops 268435456 | bytes 2097152 | tf_op jit(solution)/shard_map/pallas_call | solution.py:197
  (1 shorter events, 0.0 us)
Async XLA Ops:
  0.0 25.8 %copy-start = (bf16[128,4096]{1,0:T(8,128)(2,1)S(1)}, bf16[128,4096]{1,0:T(8,128)(2,1)}, u32[]{:S(2)}) copy-start(bf16[128,4096]{1,0:T(8,128)(2,1)} %refs_1_.5) | copy-start | bytes 3145732
  1.9 13.2 %collective-permute-start = (bf16[128,1024]{1,0:T(8,128)(2,1)S(1)}, bf16[128,1024]{1,0:T(8,128)(2,1)S(1)}, u32[]{:S(2)}, u32[]{:S(2)}) collective-permute-start(bf16[128,1024]{1,0:T(8,128)(2,1)S(1)} %constant_dynamic-update-slice_fusion.refs_2_), channel_id=1, source_target_pairs={{0,32},{8,40},{16,48},{24,56},{32,64},{40,72},{48,80},{56,88},{64,... | collective-permute-start | bytes 786440 | tf_op jit(solution)/shard_map/ppermute | solution.py:212
  4.5 21.3 %collective-permute-start.3 = (bf16[128,1024]{1,0:T(8,128)(2,1)S(1)}, bf16[128,1024]{1,0:T(8,128)(2,1)S(1)}, u32[]{:S(2)}, u32[]{:S(2)}) collective-permute-start(bf16[128,1024]{1,0:T(8,128)(2,1)S(1)} %constant_dynamic-update-slice_fusion.refs_2_), channel_id=1, source_target_pairs={{0,16},{8,24},{16,32},{24,40},{32,48},{40,56},{48,64},{56,72},{64,... | collective-permute-start | bytes 786440 | tf_op jit(solution)/shard_map/ppermute | solution.py:212
  15.2 14.0 %collective-permute-start.2 = (bf16[128,1024]{1,0:T(8,128)(2,1)S(1)}, bf16[128,1024]{1,0:T(8,128)(2,1)S(1)}, u32[]{:S(2)}, u32[]{:S(2)}) collective-permute-start(bf16[128,1024]{1,0:T(8,128)(2,1)S(1)} %get-tuple-element.13), channel_id=1, source_target_pairs={{0,24},{8,0},{16,8},{24,16},{32,56},{40,32},{48,40},{56,48},{64,88... | collective-permute-start | bytes 786440 | tf_op jit(solution)/shard_map/ppermute | solution.py:217
  17.9 12.5 %collective-permute-start.1 = (bf16[128,1024]{1,0:T(8,128)(2,1)S(1)}, bf16[128,1024]{1,0:T(8,128)(2,1)S(1)}, u32[]{:S(2)}, u32[]{:S(2)}) collective-permute-start(bf16[128,1024]{1,0:T(8,128)(2,1)S(1)} %get-tuple-element.14), channel_id=1, source_target_pairs={{0,8},{8,16},{16,24},{24,0},{32,40},{40,48},{48,56},{56,32},{64,72... | collective-permute-start | bytes 786440 | tf_op jit(solution)/shard_map/ppermute | solution.py:217
  25.8 1.0 %copy-start.1 = (f32[5,168,128]{2,1,0:T(8,128)S(1)}, f32[5,168,128]{2,1,0:T(8,128)}, u32[]{:S(2)}) copy-start(f32[5,168,128]{2,1,0:T(8,128)} %shard_map.55.refs_0_) | copy-start | bytes 1290244

commit v3 on v2

--- a/solution.py
+++ b/solution.py
@@ -17,7 +17,33 @@
 ROW = 4
 
 
-def table_kernel(docs, scales, table, *, groups, rows, backs):
+def join_kernel(keys, values, own, other, sems):
+    half = keys.shape[1]
+    copies = [
+        pltpu.make_async_copy(source, target.at[:, pl.ds(at * half, half)], sems.at[2 * number + at])
+        for number, target in enumerate((own, other))
+        for at, source in enumerate((keys, values))
+    ]
+    for copy in copies:
+        copy.start()
+    for copy in copies:
+        copy.wait()
+
+
+def join(keys, values):
+    rows, half = keys.shape
+    vmem = pl.BlockSpec(memory_space=pltpu.VMEM)
+    return pl.pallas_call(
+        join_kernel,
+        in_specs=[pl.BlockSpec(memory_space=pl.ANY)] * 2,
+        out_specs=[vmem, vmem],
+        out_shape=[jax.ShapeDtypeStruct((rows, 2 * half), keys.dtype)] * 2,
+        scratch_shapes=[pltpu.SemaphoreType.DMA((4,))],
+    )(keys, values)
+
+
+def table_kernel(docs, scales, passed_in, table, passed, *, groups, rows, backs):
+    del passed_in, passed
     first = lax.axis_index("ctx") * rows
     pieces = rows // SCALE_BLOCK
     qpos = first + lax.broadcasted_iota(jnp.int32, (8, rows), 1)
@@ -28,37 +54,44 @@
         return end, jnp.where(end <= qpos, end, start)
 
     _, start = lax.fori_loop(0, docs.shape[0], visit, (0, jnp.zeros((8, rows), jnp.int32)), unroll=8)
-    lane = lax.broadcasted_iota(jnp.int32, (1, rows), 1) // SCALE_BLOCK
+    both = jnp.concatenate([scales[0], scales[1]], axis=0)
+    place = lax.broadcasted_iota(jnp.int32, both.shape, 1)
+    lane = lax.broadcasted_iota(jnp.int32, (2 * groups, rows), 1) // SCALE_BLOCK
+    upper = lax.broadcasted_iota(jnp.int32, (2 * groups, rows), 0) < groups
     for slot, back in enumerate(backs):
         kpos = first - back * rows + lax.broadcasted_iota(jnp.int32, (rows, rows), 0)
         keep = kpos >= start[:1]
         if back == 0:
             keep = keep & (kpos <= qpos[:1])
         table[slot, :rows, :] = jnp.where(keep, 0.0, LOW)
-        for group in range(groups):
-            line = jnp.ones((1, rows), jnp.float32)
-            for piece in range(pieces):
-                block = jnp.maximum(first // SCALE_BLOCK - back * pieces + piece, 0)
-                kscale = scales[block * 2 * groups + group] * (math.log2(math.e) / math.sqrt(HEAD))
-                vscale = scales[block * 2 * groups + groups + group]
-                at = rows + group * (2 * pieces + 1) + 2 * piece
-                table[slot, at : at + 1, :] = jnp.full((1, rows), kscale, jnp.float32)
-                table[slot, at + 1 : at + 2, :] = jnp.log2(jnp.full((1, rows), vscale, jnp.float32))
-                line = jnp.where(lane == piece, vscale, line)
-            at = rows + group * (2 * pieces + 1) + 2 * pieces
-            table[slot, at : at + 1, :] = 1.0 / line
-
-
-def make_table(docs, scales, rows, groups, backs):
-    depth = rows + groups * (2 * (rows // SCALE_BLOCK) + 1)
-    depth = (depth + 7) // 8 * 8
-    smem = pl.BlockSpec(memory_space=pltpu.SMEM)
+        line = jnp.ones((2 * groups, rows), jnp.float32)
+        for piece in range(pieces):
+            block = jnp.maximum(first // SCALE_BLOCK - back * pieces + piece, 0)
+            column = jnp.sum(jnp.where(place == block, both, 0.0), axis=1, keepdims=True)
+            wide = jnp.broadcast_to(column, (2 * groups, rows))
+            at = rows + 2 * groups * piece
+            table[slot, at : at + 2 * groups, :] = jnp.where(
+                upper, wide * (math.log2(math.e) / math.sqrt(HEAD)), jnp.log2(wide)
+            )
+            line = jnp.where(lane == piece, wide, line)
+        at = rows + 2 * groups * pieces
+        table[slot, at : at + 2 * groups, :] = 1.0 / line
+
+
+def make_table(docs, scales, passed, rows, groups, backs):
+    depth = rows + 2 * groups * (rows // SCALE_BLOCK + 1)
+    vmem = pl.BlockSpec(memory_space=pltpu.VMEM)
+    anywhere = pl.BlockSpec(memory_space=pl.ANY)
     return pl.pallas_call(
         functools.partial(table_kernel, groups=groups, rows=rows, backs=backs),
-        in_specs=[smem, smem],
-        out_specs=pl.BlockSpec(memory_space=pltpu.VMEM),
-        out_shape=jax.ShapeDtypeStruct((len(backs), depth, rows), jnp.float32),
-    )(docs, scales)
+        in_specs=[pl.BlockSpec(memory_space=pltpu.SMEM), vmem, anywhere],
+        out_specs=[vmem, anywhere],
+        out_shape=[
+            jax.ShapeDtypeStruct((len(backs), depth, rows), jnp.float32),
+            jax.ShapeDtypeStruct(passed.shape, passed.dtype),
+        ],
+        input_output_aliases={2: 1},
+    )(docs, scales.transpose(1, 2, 0), passed)
 
 
 def kernel(*refs, slots, groups, rows, state, final, chunk):
@@ -90,17 +123,18 @@
     def prepare(group):
         at = group % 3
         for slot in range(count):
-            base = rows + group * (2 * pieces + 1)
             for piece in range(pieces):
                 source = pl.ds(piece * SCALE_BLOCK, SCALE_BLOCK)
                 target = pl.ds(slot * rows + piece * SCALE_BLOCK, SCALE_BLOCK)
-                kscale = table[slots[slot], base + 2 * piece : base + 2 * piece + 1, :]
+                base = rows + 2 * groups * piece + group
+                kscale = table[slots[slot], base : base + 1, :]
                 scaled = blocks[slot][source, group * HEAD : (group + 1) * HEAD].astype(jnp.float32) * kscale
                 high = scaled.astype(jnp.bfloat16)
                 kparts[at, target, :HEAD] = high
                 kparts[at, target, HEAD:] = (scaled - high.astype(jnp.float32)).astype(jnp.bfloat16)
-                bias[at, target, :] = table[slots[slot], source, :] + table[slots[slot], base + 2 * piece + 1 : base + 2 * piece + 2, :]
-            inverse = table[slots[slot], base + 2 * pieces : base + 2 * pieces + 1, :]
+                bias[at, target, :] = table[slots[slot], source, :] + table[slots[slot], base + groups : base + groups + 1, :]
+            base = rows + 2 * groups * pieces + groups + group
+            inverse = table[slots[slot], base : base + 1, :]
             high = inverse.astype(jnp.bfloat16).astype(jnp.float32)
             ones = jnp.where(deep == 0, high, jnp.where(deep == 1, inverse - high, 0.0))
             columns = pl.ds(slot * rows, rows)
@@ -220,13 +254,13 @@
 def per_device(queries, keys, values, key_value_scales, doc_lengths):
     rows = queries.shape[0]
     groups = key_value_scales.shape[2]
-    own = jnp.concatenate([keys, values], axis=1)
+    own, other = join(keys, values)
     column = lax.axis_index("ctx") % ROW
     fourth = ahead(own, 4)
-    second = ahead(own, 2)
+    table, other = make_table(doc_lengths, key_value_scales, other, rows, groups, (0, 4, 2, 3, 1))
+    second = ahead(other, 2)
     third = in_row(jnp.where(column == 0, own, fourth), ROW - 1)
     nearest = in_row(jnp.where(column < ROW - 1, own, fourth), 1)
-    table = make_table(doc_lengths, key_value_scales.reshape(-1), rows, groups, (0, 4, 2, 3, 1))
     state = attend(table, queries, (own, fourth, second), (0, 1, 2), final=False)
     state = attend(table, queries, (third,), (3,), state=state, final=False)
     return attend(table, queries, (nearest,), (4,), state=state)

time: 33.1 us -> 32.7 us (0.988)
  the two profiles are of different devices: /device:TPU:294 before, /device:TPU:288 now
where the time goes in v3:
time: 32.7 us; the launch traced here: 32.3 us
  starting transfers between devices  14.9 us (46%)
  Pallas kernels  9.46 us (29%)
  waiting for transfers between devices  3.67 us (11%)
  local copies, waits for them, and re-layouts  3.18 us (10%)
  other arithmetic  0.99 us (3%)
    ppermute x2, starting transfers between devices, ahead(): lax.ppermute(block, 'ctx', [(i, i + distance) for i in range(size - dista...  7.64 us
    ppermute x2, starting transfers between devices, in_row(): lax.ppermute(block, 'ctx', [(i, i // ROW * ROW + (i + step) % ROW) for i...  7.23 us
    pallas_call x3, Pallas kernels, attend(): pl.pallas_call(functools.partial(kernel, slots=slots, groups=groups, rows...  5.89 us
    unnamed x8, local copies, waits for them, and re-layouts  3.18 us
    ppermute x2, waiting for transfers between devices, ahead(): lax.ppermute(block, 'ctx', [(i, i + distance) for i in range(size - dista...  2.96 us
    pallas_call x1, Pallas kernels, join(): pl.pallas_call(join_kernel, in_specs=[pl.BlockSpec(memory_space=pl.ANY)]...  1.93 us
    pallas_call x1, Pallas kernels, make_table(): pl.pallas_call(functools.partial(table_kernel, groups=groups, rows=rows,...  1.63 us
    select_n x1, other arithmetic, per_device(): third = in_row(jnp.where(column == 0, own, fourth), ROW - 1)  0.99 us
  transfers between devices with their start and end apart: 4, of which 2 were waited for; matrix products, arithmetic and copies ran while one was open for 3% of the time, Pallas kernels for 16%

profile of v3, /device:TPU:288, one launch (start us, length us, event | category | flops | bytes accessed | tf_op | source)
XLA Modules:
  0.0 32.3 jit_solution(17925278463779550583)
XLA Ops:
  0.0 1.9 %shard_map.55 = (bf16[128,1024]{1,0:T(8,128)(2,1)}, bf16[128,1024]{1,0:T(8,128)(2,1)}) custom-call(bf16[128,512]{1,0:T(8,128)(2,1)} %keys.1, bf16[128,512]{1,0:T(8,128)(2,1)} %values.1), custom_call_target="tpu_custom_call" | custom-call | tf_op jit(solution)/shard_map/pallas_call | solution.py:36
  1.9 2.6 %collective-permute-start = (bf16[128,1024]{1,0:T(8,128)(2,1)}, bf16[128,1024]{1,0:T(8,128)(2,1)S(1)}, u32[]{:S(2)}, u32[]{:S(2)}) collective-permute-start(bf16[128,1024]{1,0:T(8,128)(2,1)} %get-tuple-element.15.refs_2_), channel_id=1, source_target_pairs={{0,32},{8,40},{16,48},{24,56},{32,64},{40,72},{48,80},{56,88},{64,... | collective-permute-start | bytes 786440 | tf_op jit(solution)/shard_map/ppermute | solution.py:246
  4.5 1.6 %shard_map.56 = (f32[5,168,128]{2,1,0:T(8,128)}, bf16[128,1024]{1,0:T(8,128)(2,1)}) custom-call(s32[32]{0:T(128)} %docs.1, f32[2,4,256]{2,1,0:T(4,128)} %bitcast.1, bf16[128,1024]{1,0:T(8,128)(2,1)} %get-tuple-element.13.passed_in), custom_call_target="tpu_custom_call", output_to_operand_aliasing={{1}: (2, {})} | custom-call | tf_op jit(solution)/shard_map/pallas_call | solution.py:85
  6.2 0.0 copy-start.1
  6.2 5.1 %collective-permute-start.3 = (bf16[128,1024]{1,0:T(8,128)(2,1)}, bf16[128,1024]{1,0:T(8,128)(2,1)S(1)}, u32[]{:S(2)}, u32[]{:S(2)}) collective-permute-start(bf16[128,1024]{1,0:T(8,128)(2,1)} %get-tuple-element.16), channel_id=1, source_target_pairs={{0,16},{8,24},{16,32},{24,40},{32,48},{40,56},{48,64},{56,72},{64,... | collective-permute-start | bytes 786440 | tf_op jit(solution)/shard_map/ppermute | solution.py:246
  11.2 3.0 %collective-permute-done.refs_3_ = bf16[128,1024]{1,0:T(8,128)(2,1)S(1)} collective-permute-done((bf16[128,1024]{1,0:T(8,128)(2,1)}, bf16[128,1024]{1,0:T(8,128)(2,1)S(1)}, u32[]{:S(2)}, u32[]{:S(2)}) %collective-permute-start) | collective-permute-done | bytes 262176 | tf_op jit(solution)/shard_map/ppermute | solution.py:246
  14.2 1.0 %broadcast_select_fusion = (bf16[128,1024]{1,0:T(8,128)(2,1)S(1)}, bf16[128,1024]{1,0:T(8,128)(2,1)S(1)}) fusion(bf16[128,1024]{1,0:T(8,128)(2,1)} %get-tuple-element.15.refs_2_, bf16[128,1024]{1,0:T(8,128)(2,1)S(1)} %collective-permute-done.refs_3_, pred[]{:T(512)S(6)} %eq.5, pred[]{:T(512)S(6)} %lt.10), kind=kLoop, calls=%fused_computation | loop fusion | flops 262144 | bytes 1048578 | tf_op jit(solution)/shard_map/jit(_where)/select_n | solution.py:262
  15.2 5.3 %collective-permute-start.2 = (bf16[128,1024]{1,0:T(8,128)(2,1)S(1)}, bf16[128,1024]{1,0:T(8,128)(2,1)S(1)}, u32[]{:S(2)}, u32[]{:S(2)}) collective-permute-start(bf16[128,1024]{1,0:T(8,128)(2,1)S(1)} %get-tuple-element.21), channel_id=1, source_target_pairs={{0,24},{8,0},{16,8},{24,16},{32,56},{40,32},{48,40},{56,48},{64,88... | collective-permute-start | bytes 786440 | tf_op jit(solution)/shard_map/ppermute | solution.py:251
  20.5 1.9 %collective-permute-start.1 = (bf16[128,1024]{1,0:T(8,128)(2,1)S(1)}, bf16[128,1024]{1,0:T(8,128)(2,1)S(1)}, u32[]{:S(2)}, u32[]{:S(2)}) collective-permute-start(bf16[128,1024]{1,0:T(8,128)(2,1)S(1)} %get-tuple-element.22), channel_id=1, source_target_pairs={{0,8},{8,16},{16,24},{24,0},{32,40},{40,48},{48,56},{56,32},{64,72... | collective-permute-start | bytes 786440 | tf_op jit(solution)/shard_map/ppermute | solution.py:251
  22.4 0.0 collective-permute-done.3.refs_4_
  22.4 0.0 copy-start
  22.5 1.2 %copy-done = bf16[128,4096]{1,0:T(8,128)(2,1)S(1)} copy-done((bf16[128,4096]{1,0:T(8,128)(2,1)S(1)}, bf16[128,4096]{1,0:T(8,128)(2,1)}, u32[]{:S(2)}) %copy-start) | copy-done | bytes 1048600
  23.7 0.0 copy-start.2
  23.7 1.0 %copy-done.2 = f32[5,168,128]{2,1,0:T(8,128)S(1)} copy-done((f32[5,168,128]{2,1,0:T(8,128)S(1)}, f32[5,168,128]{2,1,0:T(8,128)}, u32[]{:S(2)}) %copy-start.2) | copy-done | bytes 430104
  24.7 0.0 copy-start.3
  24.7 0.9 %copy-done.3 = bf16[128,1024]{1,0:T(8,128)(2,1)S(1)} copy-done((bf16[128,1024]{1,0:T(8,128)(2,1)S(1)}, bf16[128,1024]{1,0:T(8,128)(2,1)}, u32[]{:S(2)}) %copy-start.3) | copy-done | bytes 262168
  25.6 2.3 %shard_map.57 = (f32[4096,128]{1,0:T(8,128)S(1)}, f32[64,128]{1,0:T(8,128)S(1)}) custom-call(f32[5,168,128]{2,1,0:T(8,128)S(1)} %copy-done.2, bf16[128,4096]{1,0:T(8,128)(2,1)S(1)} %copy-done, bf16[128,1024]{1,0:T(8,128)(2,1)S(1)} %copy-done.3, bf16[128,1024]{1,0:T(8,128)(2,1)S(1)} %collective-permute-done.refs_3_, ...), custom_call_target="tpu_custom_call" | custom-call | flops 805306368 | bytes 2097152 | tf_op jit(solution)/shard_map/pallas_call | solution.py:231
  28.0 0.0 collective-permute-done.2.refs_2_
  28.0 0.0 copy-done.1
  28.0 1.3 %shard_map.58 = (f32[4096,128]{1,0:T(8,128)S(1)}, f32[64,128]{1,0:T(8,128)S(1)}) custom-call(f32[5,168,128]{2,1,0:T(8,128)S(1)} %copy-done.2, bf16[128,4096]{1,0:T(8,128)(2,1)S(1)} %copy-done.1, bf16[128,1024]{1,0:T(8,128)(2,1)S(1)} %collective-permute-done.2.refs_2_, f32[4096,128]{1,0:T(8,128)S(1)} %get-tuple-element.17.refs_3_, ...), custom_call_target="tpu_custom_call" | custom-call | flops 268435456 | bytes 2097152 | tf_op jit(solution)/shard_map/pallas_call | solution.py:231
  29.3 0.7 %collective-permute-done.1.refs_2_ = bf16[128,1024]{1,0:T(8,128)(2,1)S(1)} collective-permute-done((bf16[128,1024]{1,0:T(8,128)(2,1)S(1)}, bf16[128,1024]{1,0:T(8,128)(2,1)S(1)}, u32[]{:S(2)}, u32[]{:S(2)}) %collective-permute-start.1) | collective-permute-done | bytes 262176 | tf_op jit(solution)/shard_map/ppermute | solution.py:251
  30.0 2.3 %shard_map.59 = bf16[128,4096]{1,0:T(8,128)(2,1)} custom-call(f32[5,168,128]{2,1,0:T(8,128)S(1)} %copy-done.2, bf16[128,4096]{1,0:T(8,128)(2,1)S(1)} %copy-done.1, bf16[128,1024]{1,0:T(8,128)(2,1)S(1)} %collective-permute-done.1.refs_2_, f32[4096,128]{1,0:T(8,128)S(1)} %get-tuple-element.19.refs_3_, f32[64,128]{1,0:T(8,128)S(1)} %get-tuple-element.20.refs_4_), custom_call_target="tpu_custom_call" | custom-call | flops 268435456 | bytes 2097152 | tf_op jit(solution)/shard_map/pallas_call | solution.py:231
Async XLA Ops:
  1.9 12.3 %collective-permute-start = (bf16[128,1024]{1,0:T(8,128)(2,1)}, bf16[128,1024]{1,0:T(8,128)(2,1)S(1)}, u32[]{:S(2)}, u32[]{:S(2)}) collective-permute-start(bf16[128,1024]{1,0:T(8,128)(2,1)} %get-tuple-element.15.refs_2_), channel_id=1, source_target_pairs={{0,32},{8,40},{16,48},{24,56},{32,64},{40,72},{48,80},{56,88},{64,... | collective-permute-start | bytes 786440 | tf_op jit(solution)/shard_map/ppermute | solution.py:246
  6.2 21.8 %copy-start.1 = (bf16[128,4096]{1,0:T(8,128)(2,1)S(1)}, bf16[128,4096]{1,0:T(8,128)(2,1)}, u32[]{:S(2)}) copy-start(bf16[128,4096]{1,0:T(8,128)(2,1)} %refs_1_.5) | copy-start | bytes 3145732
  6.2 16.3 %collective-permute-start.3 = (bf16[128,1024]{1,0:T(8,128)(2,1)}, bf16[128,1024]{1,0:T(8,128)(2,1)S(1)}, u32[]{:S(2)}, u32[]{:S(2)}) collective-permute-start(bf16[128,1024]{1,0:T(8,128)(2,1)} %get-tuple-element.16), channel_id=1, source_target_pairs={{0,16},{8,24},{16,32},{24,40},{32,48},{40,56},{48,64},{56,72},{64,... | collective-permute-start | bytes 786440 | tf_op jit(solution)/shard_map/ppermute | solution.py:246
  15.2 12.8 %collective-permute-start.2 = (bf16[128,1024]{1,0:T(8,128)(2,1)S(1)}, bf16[128,1024]{1,0:T(8,128)(2,1)S(1)}, u32[]{:S(2)}, u32[]{:S(2)}) collective-permute-start(bf16[128,1024]{1,0:T(8,128)(2,1)S(1)} %get-tuple-element.21), channel_id=1, source_target_pairs={{0,24},{8,0},{16,8},{24,16},{32,56},{40,32},{48,40},{56,48},{64,88... | collective-permute-start | bytes 786440 | tf_op jit(solution)/shard_map/ppermute | solution.py:251
  20.5 9.5 %collective-permute-start.1 = (bf16[128,1024]{1,0:T(8,128)(2,1)S(1)}, bf16[128,1024]{1,0:T(8,128)(2,1)S(1)}, u32[]{:S(2)}, u32[]{:S(2)}) collective-permute-start(bf16[128,1024]{1,0:T(8,128)(2,1)S(1)} %get-tuple-element.22), channel_id=1, source_target_pairs={{0,8},{8,16},{16,24},{24,0},{32,40},{40,48},{48,56},{56,32},{64,72... | collective-permute-start | bytes 786440 | tf_op jit(solution)/shard_map/ppermute | solution.py:251
  22.4 1.2 %copy-start = (bf16[128,4096]{1,0:T(8,128)(2,1)S(1)}, bf16[128,4096]{1,0:T(8,128)(2,1)}, u32[]{:S(2)}) copy-start(bf16[128,4096]{1,0:T(8,128)(2,1)} %refs_1_.5) | copy-start | bytes 3145732
  23.7 1.0 %copy-start.2 = (f32[5,168,128]{2,1,0:T(8,128)S(1)}, f32[5,168,128]{2,1,0:T(8,128)}, u32[]{:S(2)}) copy-start(f32[5,168,128]{2,1,0:T(8,128)} %get-tuple-element.14.refs_0_) | copy-start | bytes 1290244
  24.7 0.9 %copy-start.3 = (bf16[128,1024]{1,0:T(8,128)(2,1)S(1)}, bf16[128,1024]{1,0:T(8,128)(2,1)}, u32[]{:S(2)}) copy-start(bf16[128,1024]{1,0:T(8,128)(2,1)} %get-tuple-element.15.refs_2_) | copy-start | bytes 786436

commit v4 on v3

--- a/solution.py
+++ b/solution.py
@@ -39,6 +39,7 @@
         out_specs=[vmem, vmem],
         out_shape=[jax.ShapeDtypeStruct((rows, 2 * half), keys.dtype)] * 2,
         scratch_shapes=[pltpu.SemaphoreType.DMA((4,))],
+        compiler_params=pltpu.CompilerParams(vmem_limit_bytes=4 * 2**20),
     )(keys, values)
 
 
@@ -91,6 +92,7 @@
             jax.ShapeDtypeStruct(passed.shape, passed.dtype),
         ],
         input_output_aliases={2: 1},
+        compiler_params=pltpu.CompilerParams(vmem_limit_bytes=4 * 2**20),
     )(docs, scales.transpose(1, 2, 0), passed)
 
 
@@ -234,7 +236,7 @@
         out_specs=anywhere if final else [pl.BlockSpec(memory_space=pltpu.VMEM)] * 2,
         out_shape=jax.ShapeDtypeStruct((rows, width), jnp.bfloat16) if final else state_shapes,
         scratch_shapes=scratch,
-        compiler_params=pltpu.CompilerParams(vmem_limit_bytes=40 * 2**20),
+        compiler_params=pltpu.CompilerParams(vmem_limit_bytes=24 * 2**20),
         cost_estimate=pl.CostEstimate(
             flops=4 * rows * width * span, bytes_accessed=4 * rows * width, transcendentals=heads * rows * span
         ),

time: 32.7 us -> 32.1 us (0.982)
  the two profiles are of different devices: /device:TPU:288 before, /device:TPU:251 now
where the time goes in v4:
time: 32.1 us; the launch traced here: 31.8 us
  starting transfers between devices  15.2 us (47%)
  Pallas kernels  6.76 us (21%)
  waiting for transfers between devices  5.35 us (17%)
  local copies, waits for them, and re-layouts  4.39 us (14%)
    ppermute x2, starting transfers between devices, ahead(): lax.ppermute(block, 'ctx', [(i, i + distance) for i in range(size - dista...  9.88 us
    pallas_call x3, Pallas kernels, attend(): pl.pallas_call(functools.partial(kernel, slots=slots, groups=groups, rows...  5.95 us
    ppermute x2, starting transfers between devices, in_row(): lax.ppermute(block, 'ctx', [(i, i // ROW * ROW + (i + step) % ROW) for i...  5.28 us
    unnamed x12, local copies, waits for them, and re-layouts  4.39 us
    ppermute x2, waiting for transfers between devices, in_row(): lax.ppermute(block, 'ctx', [(i, i // ROW * ROW + (i + step) % ROW) for i...  3.28 us
    ppermute x2, waiting for transfers between devices, ahead(): lax.ppermute(block, 'ctx', [(i, i + distance) for i in range(size - dista...  2.07 us
    pallas_call x1, Pallas kernels, make_table(): pl.pallas_call(functools.partial(table_kernel, groups=groups, rows=rows,...  0.71 us
  transfers between devices with their start and end apart: 4, of which 2 were waited for; matrix products, arithmetic and copies ran while one was open for 0% of the time, Pallas kernels for 14%

profile of v4, /device:TPU:251, one launch (start us, length us, event | category | flops | bytes accessed | tf_op | source)
XLA Modules:
  0.0 31.8 jit_solution(4485922813031438782)
XLA Ops:
  0.0 0.0 copy-start.2
  0.0 0.9 %copy-done.2 = bf16[128,512]{1,0:T(8,128)(2,1)S(1)} copy-done((bf16[128,512]{1,0:T(8,128)(2,1)S(1)}, bf16[128,512]{1,0:T(8,128)(2,1)}, u32[]{:S(2)}) %copy-start.2) | copy-done | bytes 131096
  0.9 0.0 copy-start.3
  0.9 0.9 %copy-done.3 = bf16[128,512]{1,0:T(8,128)(2,1)S(1)} copy-done((bf16[128,512]{1,0:T(8,128)(2,1)S(1)}, bf16[128,512]{1,0:T(8,128)(2,1)}, u32[]{:S(2)}) %copy-start.3) | copy-done | bytes 131096
  1.8 0.1 shard_map.55
  1.9 6.0 %collective-permute-start = (bf16[128,1024]{1,0:T(8,128)(2,1)S(1)}, bf16[128,1024]{1,0:T(8,128)(2,1)S(1)}, u32[]{:S(2)}, u32[]{:S(2)}) collective-permute-start(bf16[128,1024]{1,0:T(8,128)(2,1)S(1)} %get-tuple-element.15.refs_2_), channel_id=1, source_target_pairs={{0,32},{8,40},{16,48},{24,56},{32,64},{40,72},{48,80},{56,88},{64,... | collective-permute-start | bytes 786440 | tf_op jit(solution)/shard_map/ppermute | solution.py:248
  7.9 0.0 copy-start.4
  7.9 0.7 %copy-done.4 = f32[256,2,4]{0,2,1:T(4,128)S(1)} copy-done((f32[256,2,4]{0,2,1:T(4,128)S(1)}, f32[256,2,4]{0,2,1:T(4,128)}, u32[]{:S(2)}) %copy-start.4) | copy-done | bytes 8216
  8.6 0.0 copy-start.5
  8.6 0.7 %copy-done.5 = s32[32]{0:T(128)S(1)} copy-done((s32[32]{0:T(128)S(1)}, s32[32]{0:T(128)}, u32[]{:S(2)}) %copy-start.5) | copy-done | bytes 152
  9.3 0.7 %shard_map.56 = (f32[5,168,128]{2,1,0:T(8,128)S(1)}, bf16[128,1024]{1,0:T(8,128)(2,1)S(1)}) custom-call(s32[32]{0:T(128)S(1)} %copy-done.5, f32[2,4,256]{2,1,0:T(4,128)S(1)} %bitcast.1, bf16[128,1024]{1,0:T(8,128)(2,1)S(1)} %get-tuple-element.13.passed_in), custom_call_target="tpu_custom_call", output_to_operand_aliasing={{1}: (2, {})} | custom-call | tf_op jit(solution)/shard_map/pallas_call | solution.py:86
  10.0 0.0 copy-start.1
  10.0 3.9 %collective-permute-start.3 = (bf16[128,1024]{1,0:T(8,128)(2,1)S(1)}, bf16[128,1024]{1,0:T(8,128)(2,1)S(1)}, u32[]{:S(2)}, u32[]{:S(2)}) collective-permute-start(bf16[128,1024]{1,0:T(8,128)(2,1)S(1)} %get-tuple-element.16), channel_id=1, source_target_pairs={{0,16},{8,24},{16,32},{24,40},{32,48},{40,56},{48,64},{56,72},{64,... | collective-permute-start | bytes 786440 | tf_op jit(solution)/shard_map/ppermute | solution.py:248
  13.9 0.0 collective-permute-done.refs_3_
  14.0 3.1 %collective-permute-start.2 = (bf16[128,1024]{1,0:T(8,128)(2,1)S(1)}, bf16[128,1024]{1,0:T(8,128)(2,1)S(1)}, u32[]{:S(2)}, u32[]{:S(2)}) collective-permute-start(bf16[128,1024]{1,0:T(8,128)(2,1)S(1)} %get-tuple-element.21), channel_id=1, source_target_pairs={{0,24},{8,0},{16,8},{24,16},{32,56},{40,32},{48,40},{56,48},{64,88... | collective-permute-start | bytes 786440 | tf_op jit(solution)/shard_map/ppermute | solution.py:253
  17.0 2.2 %collective-permute-start.1 = (bf16[128,1024]{1,0:T(8,128)(2,1)S(1)}, bf16[128,1024]{1,0:T(8,128)(2,1)S(1)}, u32[]{:S(2)}, u32[]{:S(2)}) collective-permute-start(bf16[128,1024]{1,0:T(8,128)(2,1)S(1)} %get-tuple-element.22), channel_id=1, source_target_pairs={{0,8},{8,16},{16,24},{24,0},{32,40},{40,48},{48,56},{56,32},{64,72... | collective-permute-start | bytes 786440 | tf_op jit(solution)/shard_map/ppermute | solution.py:253
  19.3 2.1 %collective-permute-done.3.refs_4_ = bf16[128,1024]{1,0:T(8,128)(2,1)S(1)} collective-permute-done((bf16[128,1024]{1,0:T(8,128)(2,1)S(1)}, bf16[128,1024]{1,0:T(8,128)(2,1)S(1)}, u32[]{:S(2)}, u32[]{:S(2)}) %collective-permute-start.3) | collective-permute-done | bytes 262176 | tf_op jit(solution)/shard_map/ppermute | solution.py:248
  21.3 1.2 %copy-done = bf16[128,4096]{1,0:T(8,128)(2,1)S(1)} copy-done((bf16[128,4096]{1,0:T(8,128)(2,1)S(1)}, bf16[128,4096]{1,0:T(8,128)(2,1)}, u32[]{:S(2)}) %copy-start) | copy-done | bytes 1048600
  22.6 2.4 %shard_map.57 = (f32[4096,128]{1,0:T(8,128)S(1)}, f32[64,128]{1,0:T(8,128)S(1)}) custom-call(f32[5,168,128]{2,1,0:T(8,128)S(1)} %get-tuple-element.14.refs_0_, bf16[128,4096]{1,0:T(8,128)(2,1)S(1)} %copy-done, bf16[128,1024]{1,0:T(8,128)(2,1)S(1)} %get-tuple-element.15.refs_2_, bf16[128,1024]{1,0:T(8,128)(2,1)S(1)} %collective-permute-done.refs_3_, ...), custom_call_target="tpu_custom_call" | custom-call | flops 805306368 | bytes 2097152 | tf_op jit(solution)/shard_map/pallas_call | solution.py:233
  25.0 3.3 %collective-permute-done.2.refs_2_ = bf16[128,1024]{1,0:T(8,128)(2,1)S(1)} collective-permute-done((bf16[128,1024]{1,0:T(8,128)(2,1)S(1)}, bf16[128,1024]{1,0:T(8,128)(2,1)S(1)}, u32[]{:S(2)}, u32[]{:S(2)}) %collective-permute-start.2) | collective-permute-done | bytes 262176 | tf_op jit(solution)/shard_map/ppermute | solution.py:253
  28.2 0.0 copy-done.1
  28.2 1.2 %shard_map.58 = (f32[4096,128]{1,0:T(8,128)S(1)}, f32[64,128]{1,0:T(8,128)S(1)}) custom-call(f32[5,168,128]{2,1,0:T(8,128)S(1)} %get-tuple-element.14.refs_0_, bf16[128,4096]{1,0:T(8,128)(2,1)S(1)} %copy-done.1, bf16[128,1024]{1,0:T(8,128)(2,1)S(1)} %collective-permute-done.2.refs_2_, f32[4096,128]{1,0:T(8,128)S(1)} %get-tuple-element.17.refs_3_, ...), custom_call_target="tpu_custom_call" | custom-call | flops 268435456 | bytes 2097152 | tf_op jit(solution)/shard_map/pallas_call | solution.py:233
  29.5 0.0 collective-permute-done.1.refs_2_
  29.5 2.3 %shard_map.59 = bf16[128,4096]{1,0:T(8,128)(2,1)} custom-call(f32[5,168,128]{2,1,0:T(8,128)S(1)} %get-tuple-element.14.refs_0_, bf16[128,4096]{1,0:T(8,128)(2,1)S(1)} %copy-done.1, bf16[128,1024]{1,0:T(8,128)(2,1)S(1)} %collective-permute-done.1.refs_2_, f32[4096,128]{1,0:T(8,128)S(1)} %get-tuple-element.19.refs_3_, f32[64,128]{1,0:T(8,128)S(1)} %get-tuple-element.20.refs_4_), custom_call_target="tpu_custom_call" | custom-call | flops 268435456 | bytes 2097152 | tf_op jit(solution)/shard_map/pallas_call | solution.py:233
  (2 shorter events, 0.0 us)
Async XLA Ops:
  0.0 0.9 %copy-start.2 = (bf16[128,512]{1,0:T(8,128)(2,1)S(1)}, bf16[128,512]{1,0:T(8,128)(2,1)}, u32[]{:S(2)}) copy-start(bf16[128,512]{1,0:T(8,128)(2,1)} %keys.1) | copy-start | bytes 393220
  0.9 0.9 %copy-start.3 = (bf16[128,512]{1,0:T(8,128)(2,1)S(1)}, bf16[128,512]{1,0:T(8,128)(2,1)}, u32[]{:S(2)}) copy-start(bf16[128,512]{1,0:T(8,128)(2,1)} %values.1) | copy-start | bytes 393220
  1.9 12.0 %collective-permute-start = (bf16[128,1024]{1,0:T(8,128)(2,1)S(1)}, bf16[128,1024]{1,0:T(8,128)(2,1)S(1)}, u32[]{:S(2)}, u32[]{:S(2)}) collective-permute-start(bf16[128,1024]{1,0:T(8,128)(2,1)S(1)} %get-tuple-element.15.refs_2_), channel_id=1, source_target_pairs={{0,32},{8,40},{16,48},{24,56},{32,64},{40,72},{48,80},{56,88},{64,... | collective-permute-start | bytes 786440 | tf_op jit(solution)/shard_map/ppermute | solution.py:248
  7.9 0.7 %copy-start.4 = (f32[256,2,4]{0,2,1:T(4,128)S(1)}, f32[256,2,4]{0,2,1:T(4,128)}, u32[]{:S(2)}) copy-start(f32[256,2,4]{0,2,1:T(4,128)} %param.8) | copy-start | bytes 24580
  8.6 0.7 %copy-start.5 = (s32[32]{0:T(128)S(1)}, s32[32]{0:T(128)}, u32[]{:S(2)}) copy-start(s32[32]{0:T(128)} %docs.1) | copy-start | bytes 388
  10.0 18.3 %copy-start.1 = (bf16[128,4096]{1,0:T(8,128)(2,1)S(1)}, bf16[128,4096]{1,0:T(8,128)(2,1)}, u32[]{:S(2)}) copy-start(bf16[128,4096]{1,0:T(8,128)(2,1)} %refs_1_.5) | copy-start | bytes 3145732
  10.0 11.3 %collective-permute-start.3 = (bf16[128,1024]{1,0:T(8,128)(2,1)S(1)}, bf16[128,1024]{1,0:T(8,128)(2,1)S(1)}, u32[]{:S(2)}, u32[]{:S(2)}) collective-permute-start(bf16[128,1024]{1,0:T(8,128)(2,1)S(1)} %get-tuple-element.16), channel_id=1, source_target_pairs={{0,16},{8,24},{16,32},{24,40},{32,48},{40,56},{48,64},{56,72},{64,... | collective-permute-start | bytes 786440 | tf_op jit(solution)/shard_map/ppermute | solution.py:248
  14.0 14.3 %collective-permute-start.2 = (bf16[128,1024]{1,0:T(8,128)(2,1)S(1)}, bf16[128,1024]{1,0:T(8,128)(2,1)S(1)}, u32[]{:S(2)}, u32[]{:S(2)}) collective-permute-start(bf16[128,1024]{1,0:T(8,128)(2,1)S(1)} %get-tuple-element.21), channel_id=1, source_target_pairs={{0,24},{8,0},{16,8},{24,16},{32,56},{40,32},{48,40},{56,48},{64,88... | collective-permute-start | bytes 786440 | tf_op jit(solution)/shard_map/ppermute | solution.py:253
  17.0 12.5 %collective-permute-start.1 = (bf16[128,1024]{1,0:T(8,128)(2,1)S(1)}, bf16[128,1024]{1,0:T(8,128)(2,1)S(1)}, u32[]{:S(2)}, u32[]{:S(2)}) collective-permute-start(bf16[128,1024]{1,0:T(8,128)(2,1)S(1)} %get-tuple-element.22), channel_id=1, source_target_pairs={{0,8},{8,16},{16,24},{24,0},{32,40},{40,48},{48,56},{56,32},{64,72... | collective-permute-start | bytes 786440 | tf_op jit(solution)/shard_map/ppermute | solution.py:253
  21.3 1.2 %copy-start = (bf16[128,4096]{1,0:T(8,128)(2,1)S(1)}, bf16[128,4096]{1,0:T(8,128)(2,1)}, u32[]{:S(2)}) copy-start(bf16[128,4096]{1,0:T(8,128)(2,1)} %refs_1_.5) | copy-start | bytes 3145732

commit v5 on v4

--- a/solution.py
+++ b/solution.py
@@ -17,11 +17,10 @@
 ROW = 4
 
 
-def join_kernel(keys, values, own, other, sems):
+def join_kernel(keys, values, own, sems):
     half = keys.shape[1]
     copies = [
-        pltpu.make_async_copy(source, target.at[:, pl.ds(at * half, half)], sems.at[2 * number + at])
-        for number, target in enumerate((own, other))
+        pltpu.make_async_copy(source, own.at[:, pl.ds(at * half, half)], sems.at[at])
         for at, source in enumerate((keys, values))
     ]
     for copy in copies:
@@ -32,19 +31,42 @@
 
 def join(keys, values):
     rows, half = keys.shape
+    far = [pltpu.with_memory_space_constraint(x, pltpu.HBM) for x in (keys, values)]
+    return pl.pallas_call(
+        join_kernel,
+        in_specs=[pl.BlockSpec(memory_space=pltpu.HBM)] * 2,
+        out_specs=pl.BlockSpec(memory_space=pltpu.VMEM),
+        out_shape=pltpu.VMEM((rows, 2 * half), keys.dtype),
+        scratch_shapes=[pltpu.SemaphoreType.DMA((2,))],
+        compiler_params=pltpu.CompilerParams(vmem_limit_bytes=4 * 2**20),
+    )(*far)
+
+
+def pick_kernel(own, far, to_left, to_right):
+    column = lax.rem(lax.axis_index("ctx"), ROW)
+    mine, other = own[...], far[...]
+    to_left[...] = jnp.where(column == 0, mine, other)
+    to_right[...] = jnp.where(column < ROW - 1, mine, other)
+
+
+def pick(own, far):
     vmem = pl.BlockSpec(memory_space=pltpu.VMEM)
     return pl.pallas_call(
-        join_kernel,
-        in_specs=[pl.BlockSpec(memory_space=pl.ANY)] * 2,
-        out_specs=[vmem, vmem],
-        out_shape=[jax.ShapeDtypeStruct((rows, 2 * half), keys.dtype)] * 2,
-        scratch_shapes=[pltpu.SemaphoreType.DMA((4,))],
+        pick_kernel,
+        in_specs=[vmem] * 2,
+        out_specs=[vmem] * 2,
+        out_shape=[pltpu.VMEM(own.shape, own.dtype)] * 2,
         compiler_params=pltpu.CompilerParams(vmem_limit_bytes=4 * 2**20),
-    )(keys, values)
-
-
-def table_kernel(docs, scales, passed_in, table, passed, *, groups, rows, backs):
-    del passed_in, passed
+    )(own, far)
+
+
+def setup_kernel(docs_far, scales_far, queries, table, near, docs, scales, sems, *, groups, rows, backs):
+    pairs = ((docs_far, docs), (scales_far, scales), (queries, near))
+    copies = [pltpu.make_async_copy(source, target, sems.at[at]) for at, (source, target) in enumerate(pairs)]
+    for copy in copies:
+        copy.start()
+    copies[0].wait()
+    copies[1].wait()
     first = lax.axis_index("ctx") * rows
     pieces = rows // SCALE_BLOCK
     qpos = first + lax.broadcasted_iota(jnp.int32, (8, rows), 1)
@@ -77,23 +99,29 @@
             line = jnp.where(lane == piece, wide, line)
         at = rows + 2 * groups * pieces
         table[slot, at : at + 2 * groups, :] = 1.0 / line
-
-
-def make_table(docs, scales, passed, rows, groups, backs):
+    copies[2].wait()
+
+
+def setup(docs, scales, queries, groups, backs):
+    rows = queries.shape[0]
     depth = rows + 2 * groups * (rows // SCALE_BLOCK + 1)
-    vmem = pl.BlockSpec(memory_space=pltpu.VMEM)
-    anywhere = pl.BlockSpec(memory_space=pl.ANY)
+    scales = scales.transpose(1, 2, 0)
+    far = [pltpu.with_memory_space_constraint(x, pltpu.HBM) for x in (docs, scales, queries)]
     return pl.pallas_call(
-        functools.partial(table_kernel, groups=groups, rows=rows, backs=backs),
-        in_specs=[pl.BlockSpec(memory_space=pltpu.SMEM), vmem, anywhere],
-        out_specs=[vmem, anywhere],
+        functools.partial(setup_kernel, groups=groups, rows=rows, backs=backs),
+        in_specs=[pl.BlockSpec(memory_space=pltpu.HBM)] * 3,
+        out_specs=[pl.BlockSpec(memory_space=pltpu.VMEM)] * 2,
         out_shape=[
-            jax.ShapeDtypeStruct((len(backs), depth, rows), jnp.float32),
-            jax.ShapeDtypeStruct(passed.shape, passed.dtype),
+            pltpu.VMEM((len(backs), depth, rows), jnp.float32),
+            pltpu.VMEM(queries.shape, queries.dtype),
         ],
-        input_output_aliases={2: 1},
+        scratch_shapes=[
+            pltpu.SMEM(docs.shape, docs.dtype),
+            pltpu.VMEM(scales.shape, scales.dtype),
+            pltpu.SemaphoreType.DMA((3,)),
+        ],
         compiler_params=pltpu.CompilerParams(vmem_limit_bytes=4 * 2**20),
-    )(docs, scales.transpose(1, 2, 0), passed)
+    )(*far)
 
 
 def kernel(*refs, slots, groups, rows, state, final, chunk):
@@ -208,9 +236,8 @@
             send(group).wait()
 
 
-def attend(table, queries, blocks, slots, state=None, final=True, chunk=CHUNK):
+def attend(table, queries, blocks, groups, slots, state=None, final=True, chunk=CHUNK):
     rows, width = queries.shape
-    groups = blocks[0].shape[1] // (2 * HEAD)
     count = len(slots)
     span = count * rows
     heads = width // HEAD
@@ -254,18 +281,17 @@
 
 
 def per_device(queries, keys, values, key_value_scales, doc_lengths):
-    rows = queries.shape[0]
     groups = key_value_scales.shape[2]
-    own, other = join(keys, values)
-    column = lax.axis_index("ctx") % ROW
+    own = join(keys, values)
     fourth = ahead(own, 4)
-    table, other = make_table(doc_lengths, key_value_scales, other, rows, groups, (0, 4, 2, 3, 1))
-    second = ahead(other, 2)
-    third = in_row(jnp.where(column == 0, own, fourth), ROW - 1)
-    nearest = in_row(jnp.where(column < ROW - 1, own, fourth), 1)
-    state = attend(table, queries, (own, fourth, second), (0, 1, 2), final=False)
-    state = attend(table, queries, (third,), (3,), state=state, final=False)
-    return attend(table, queries, (nearest,), (4,), state=state)
+    second = ahead(own, 2)
+    to_left, to_right = pick(own, fourth)
+    nearest = in_row(to_right, 1)
+    third = in_row(to_left, ROW - 1)
+    table, near = setup(doc_lengths, key_value_scales, queries, groups, (0, 4, 2, 1, 3))
+    state = attend(table, near, (own, fourth, second), groups, (0, 1, 2), final=False)
+    state = attend(table, near, (nearest,), groups, (3,), state=state, final=False)
+    return attend(table, near, (third,), groups, (4,), state=state)
 
 
 def solution(mesh):

time: 32.1 us -> 30.7 us (0.956)
  the two profiles are of different devices: /device:TPU:251 before, /device:TPU:288 now
where the time goes in v5:
time: 30.7 us; the launch traced here: 30.3 us
  starting transfers between devices  15.3 us (50%)
  Pallas kernels  8.3 us (27%)
  waiting for transfers between devices  6.69 us (22%)
    ppermute x2, starting transfers between devices, in_row(): lax.ppermute(block, 'ctx', [(i, i // ROW * ROW + (i + step) % ROW) for i...  7.73 us
    ppermute x2, starting transfers between devices, ahead(): lax.ppermute(block, 'ctx', [(i, i + distance) for i in range(size - dista...  7.52 us
    pallas_call x3, Pallas kernels, attend(): pl.pallas_call(functools.partial(kernel, slots=slots, groups=groups, rows...  5.97 us
    ppermute x2, waiting for transfers between devices, ahead(): lax.ppermute(block, 'ctx', [(i, i + distance) for i in range(size - dista...  4.52 us
    ppermute x2, waiting for transfers between devices, in_row(): lax.ppermute(block, 'ctx', [(i, i // ROW * ROW + (i + step) % ROW) for i...  2.17 us
    pallas_call x1, Pallas kernels, setup(): pl.pallas_call(functools.partial(setup_kernel, groups=groups, rows=rows,...  1.27 us
    pallas_call x1, Pallas kernels, join(): pl.pallas_call(join_kernel, in_specs=[pl.BlockSpec(memory_space=pltpu.HBM...  0.98 us
  transfers between devices with their start and end apart: 4, of which 2 were waited for; matrix products, arithmetic and copies ran while one was open for 0% of the time, Pallas kernels for 16%

profile of v5, /device:TPU:288, one launch (start us, length us, event | category | flops | bytes accessed | tf_op | source)
XLA Modules:
  0.0 30.3 jit_solution(8745673475137620399)
XLA Ops:
  0.0 1.0 %shard_map.56.own.refs_2_ = bf16[128,1024]{1,0:T(8,128)(2,1)S(1)} custom-call(bf16[128,512]{1,0:T(8,128)(2,1)} %keys.1, bf16[128,512]{1,0:T(8,128)(2,1)} %values.1), custom_call_target="tpu_custom_call" | custom-call | tf_op jit(solution)/shard_map/pallas_call | solution.py:35
  1.0 2.6 %collective-permute-start = (bf16[128,1024]{1,0:T(8,128)(2,1)S(1)}, bf16[128,1024]{1,0:T(8,128)(2,1)S(1)}, u32[]{:S(2)}, u32[]{:S(2)}) collective-permute-start(bf16[128,1024]{1,0:T(8,128)(2,1)S(1)} %shard_map.56.own.refs_2_), channel_id=1, source_target_pairs={{0,32},{8,40},{16,48},{24,56},{32,64},{40,72},{48,80},{56,88},{64,... | collective-permute-start | bytes 786440 | tf_op jit(solution)/shard_map/ppermute | solution.py:275
  3.6 4.9 %collective-permute-start.3 = (bf16[128,1024]{1,0:T(8,128)(2,1)S(1)}, bf16[128,1024]{1,0:T(8,128)(2,1)S(1)}, u32[]{:S(2)}, u32[]{:S(2)}) collective-permute-start(bf16[128,1024]{1,0:T(8,128)(2,1)S(1)} %shard_map.56.own.refs_2_), channel_id=1, source_target_pairs={{0,16},{8,24},{16,32},{24,40},{32,48},{40,56},{48,64},{56,72},{64,... | collective-permute-start | bytes 786440 | tf_op jit(solution)/shard_map/ppermute | solution.py:275
  8.5 4.5 %collective-permute-done.far.refs_3_ = bf16[128,1024]{1,0:T(8,128)(2,1)S(1)} collective-permute-done((bf16[128,1024]{1,0:T(8,128)(2,1)S(1)}, bf16[128,1024]{1,0:T(8,128)(2,1)S(1)}, u32[]{:S(2)}, u32[]{:S(2)}) %collective-permute-start) | collective-permute-done | bytes 262176 | tf_op jit(solution)/shard_map/ppermute | solution.py:275
  13.0 0.1 shard_map.57
  13.1 3.4 %collective-permute-start.2 = (bf16[128,1024]{1,0:T(8,128)(2,1)S(1)}, bf16[128,1024]{1,0:T(8,128)(2,1)S(1)}, u32[]{:S(2)}, u32[]{:S(2)}) collective-permute-start(bf16[128,1024]{1,0:T(8,128)(2,1)S(1)} %get-tuple-element.16), channel_id=1, source_target_pairs={{0,8},{8,16},{16,24},{24,0},{32,40},{40,48},{48,56},{56,32},{64,72... | collective-permute-start | bytes 786440 | tf_op jit(solution)/shard_map/ppermute | solution.py:280
  16.5 4.3 %collective-permute-start.1 = (bf16[128,1024]{1,0:T(8,128)(2,1)S(1)}, bf16[128,1024]{1,0:T(8,128)(2,1)S(1)}, u32[]{:S(2)}, u32[]{:S(2)}) collective-permute-start(bf16[128,1024]{1,0:T(8,128)(2,1)S(1)} %get-tuple-element.15), channel_id=1, source_target_pairs={{0,24},{8,0},{16,8},{24,16},{32,56},{40,32},{48,40},{56,48},{64,88... | collective-permute-start | bytes 786440 | tf_op jit(solution)/shard_map/ppermute | solution.py:280
  20.9 1.3 %shard_map.55 = (f32[5,168,128]{2,1,0:T(8,128)S(1)}, bf16[128,4096]{1,0:T(8,128)(2,1)S(1)}) custom-call(s32[32]{0:T(128)} %docs_far.1, f32[2,4,256]{2,1,0:T(4,128)} %bitcast.1, bf16[128,4096]{1,0:T(8,128)(2,1)} %queries.1), custom_call_target="tpu_custom_call" | custom-call | tf_op jit(solution)/shard_map/pallas_call | solution.py:110
  22.1 0.0 collective-permute-done.3.refs_4_
  22.2 2.4 %shard_map.58 = (f32[4096,128]{1,0:T(8,128)S(1)}, f32[64,128]{1,0:T(8,128)S(1)}) custom-call(f32[5,168,128]{2,1,0:T(8,128)S(1)} %get-tuple-element.13.refs_0_, bf16[128,4096]{1,0:T(8,128)(2,1)S(1)} %get-tuple-element.14.refs_1_, bf16[128,1024]{1,0:T(8,128)(2,1)S(1)} %shard_map.56.own.refs_2_, bf16[128,1024]{1,0:T(8,128)(2,1)S(1)} %collective-permute-done.far.refs_3_, ...), custom_call_target="tpu_custom_call" | custom-call | flops 805306368 | bytes 2097152 | tf_op jit(solution)/shard_map/pallas_call | solution.py:260
  24.6 2.2 %collective-permute-done.2.refs_2_ = bf16[128,1024]{1,0:T(8,128)(2,1)S(1)} collective-permute-done((bf16[128,1024]{1,0:T(8,128)(2,1)S(1)}, bf16[128,1024]{1,0:T(8,128)(2,1)S(1)}, u32[]{:S(2)}, u32[]{:S(2)}) %collective-permute-start.2) | collective-permute-done | bytes 262176 | tf_op jit(solution)/shard_map/ppermute | solution.py:280
  26.7 1.2 %shard_map.59 = (f32[4096,128]{1,0:T(8,128)S(1)}, f32[64,128]{1,0:T(8,128)S(1)}) custom-call(f32[5,168,128]{2,1,0:T(8,128)S(1)} %get-tuple-element.13.refs_0_, bf16[128,4096]{1,0:T(8,128)(2,1)S(1)} %get-tuple-element.14.refs_1_, bf16[128,1024]{1,0:T(8,128)(2,1)S(1)} %collective-permute-done.2.refs_2_, f32[4096,128]{1,0:T(8,128)S(1)} %get-tuple-element.17.refs_3_, ...), custom_call_target="tpu_custom_call" | custom-call | flops 268435456 | bytes 2097152 | tf_op jit(solution)/shard_map/pallas_call | solution.py:260
  28.0 0.0 collective-permute-done.1.refs_2_
  28.0 2.3 %shard_map.60 = bf16[128,4096]{1,0:T(8,128)(2,1)} custom-call(f32[5,168,128]{2,1,0:T(8,128)S(1)} %get-tuple-element.13.refs_0_, bf16[128,4096]{1,0:T(8,128)(2,1)S(1)} %get-tuple-element.14.refs_1_, bf16[128,1024]{1,0:T(8,128)(2,1)S(1)} %collective-permute-done.1.refs_2_, f32[4096,128]{1,0:T(8,128)S(1)} %get-tuple-element.19.refs_3_, ...), custom_call_target="tpu_custom_call" | custom-call | flops 268435456 | bytes 2097152 | tf_op jit(solution)/shard_map/pallas_call | solution.py:260
Async XLA Ops:
  1.0 12.0 %collective-permute-start = (bf16[128,1024]{1,0:T(8,128)(2,1)S(1)}, bf16[128,1024]{1,0:T(8,128)(2,1)S(1)}, u32[]{:S(2)}, u32[]{:S(2)}) collective-permute-start(bf16[128,1024]{1,0:T(8,128)(2,1)S(1)} %shard_map.56.own.refs_2_), channel_id=1, source_target_pairs={{0,32},{8,40},{16,48},{24,56},{32,64},{40,72},{48,80},{56,88},{64,... | collective-permute-start | bytes 786440 | tf_op jit(solution)/shard_map/ppermute | solution.py:275
  3.6 18.6 %collective-permute-start.3 = (bf16[128,1024]{1,0:T(8,128)(2,1)S(1)}, bf16[128,1024]{1,0:T(8,128)(2,1)S(1)}, u32[]{:S(2)}, u32[]{:S(2)}) collective-permute-start(bf16[128,1024]{1,0:T(8,128)(2,1)S(1)} %shard_map.56.own.refs_2_), channel_id=1, source_target_pairs={{0,16},{8,24},{16,32},{24,40},{32,48},{40,56},{48,64},{56,72},{64,... | collective-permute-start | bytes 786440 | tf_op jit(solution)/shard_map/ppermute | solution.py:275
  13.1 13.6 %collective-permute-start.2 = (bf16[128,1024]{1,0:T(8,128)(2,1)S(1)}, bf16[128,1024]{1,0:T(8,128)(2,1)S(1)}, u32[]{:S(2)}, u32[]{:S(2)}) collective-permute-start(bf16[128,1024]{1,0:T(8,128)(2,1)S(1)} %get-tuple-element.16), channel_id=1, source_target_pairs={{0,8},{8,16},{16,24},{24,0},{32,40},{40,48},{48,56},{56,32},{64,72... | collective-permute-start | bytes 786440 | tf_op jit(solution)/shard_map/ppermute | solution.py:280
  16.5 11.5 %collective-permute-start.1 = (bf16[128,1024]{1,0:T(8,128)(2,1)S(1)}, bf16[128,1024]{1,0:T(8,128)(2,1)S(1)}, u32[]{:S(2)}, u32[]{:S(2)}) collective-permute-start(bf16[128,1024]{1,0:T(8,128)(2,1)S(1)} %get-tuple-element.15), channel_id=1, source_target_pairs={{0,24},{8,0},{16,8},{24,16},{32,56},{40,32},{48,40},{56,48},{64,88... | collective-permute-start | bytes 786440 | tf_op jit(solution)/shard_map/ppermute | solution.py:280

commit v6 on v5

--- a/solution.py
+++ b/solution.py
@@ -42,11 +42,11 @@
     )(*far)
 
 
-def pick_kernel(own, far, to_left, to_right):
+def pick_kernel(own, far, inner, outer):
     column = lax.rem(lax.axis_index("ctx"), ROW)
     mine, other = own[...], far[...]
-    to_left[...] = jnp.where(column == 0, mine, other)
-    to_right[...] = jnp.where(column < ROW - 1, mine, other)
+    inner[...] = jnp.where(lax.rem(column, 2) == 0, mine, other)
+    outer[...] = jnp.where(column < 2, mine, other)
 
 
 def pick(own, far):
@@ -81,10 +81,13 @@
     place = lax.broadcasted_iota(jnp.int32, both.shape, 1)
     lane = lax.broadcasted_iota(jnp.int32, (2 * groups, rows), 1) // SCALE_BLOCK
     upper = lax.broadcasted_iota(jnp.int32, (2 * groups, rows), 0) < groups
-    for slot, back in enumerate(backs):
+    even = lax.rem(lax.axis_index("ctx"), 2) == 0
+    for slot, (back, odd_back) in enumerate(backs):
+        if back != odd_back:
+            back = jnp.where(even, back, odd_back)
         kpos = first - back * rows + lax.broadcasted_iota(jnp.int32, (rows, rows), 0)
         keep = kpos >= start[:1]
-        if back == 0:
+        if slot == 0:
             keep = keep & (kpos <= qpos[:1])
         table[slot, :rows, :] = jnp.where(keep, 0.0, LOW)
         line = jnp.ones((2 * groups, rows), jnp.float32)
@@ -275,9 +278,9 @@
     return lax.ppermute(block, "ctx", [(i, i + distance) for i in range(size - distance)])
 
 
-def in_row(block, step):
+def in_row(block, places):
     size = lax.axis_size("ctx")
-    return lax.ppermute(block, "ctx", [(i, i // ROW * ROW + (i + step) % ROW) for i in range(size)])
+    return lax.ppermute(block, "ctx", [(i, i // ROW * ROW + places[i % ROW]) for i in range(size)])
 
 
 def per_device(queries, keys, values, key_value_scales, doc_lengths):
@@ -285,13 +288,14 @@
     own = join(keys, values)
     fourth = ahead(own, 4)
     second = ahead(own, 2)
-    to_left, to_right = pick(own, fourth)
-    nearest = in_row(to_right, 1)
-    third = in_row(to_left, ROW - 1)
-    table, near = setup(doc_lengths, key_value_scales, queries, groups, (0, 4, 2, 1, 3))
+    inner, outer = pick(own, fourth)
+    inner = in_row(inner, (1, 0, 3, 2))
+    outer = in_row(outer, (3, 2, 1, 0))
+    backs = ((0, 0), (4, 4), (2, 2), (3, 1), (1, 3))
+    table, near = setup(doc_lengths, key_value_scales, queries, groups, backs)
     state = attend(table, near, (own, fourth, second), groups, (0, 1, 2), final=False)
-    state = attend(table, near, (nearest,), groups, (3,), state=state, final=False)
-    return attend(table, near, (third,), groups, (4,), state=state)
+    state = attend(table, near, (inner,), groups, (3,), state=state, final=False)
+    return attend(table, near, (outer,), groups, (4,), state=state)
 
 
 def solution(mesh):

time: 30.7 us -> 29.4 us (0.958)
  waiting for transfers between devices: 6.69 us -> 4.7 us
  starting transfers between devices: 15.3 us -> 16.1 us
    ppermute x2, waiting for transfers between devices: 2.17 us -> 0.18 us  [in_row(): lax.ppermute(block, 'ctx', [(i, i // ROW * ROW + places[i % ROW]) for i i...]
    ppermute x2, starting transfers between devices: 7.73 us -> 8.55 us  [in_row(): lax.ppermute(block, 'ctx', [(i, i // ROW * ROW + places[i % ROW]) for i i...]
  transfers between devices with their start and end apart: 4 -> 4, of which waited for: 2 -> 2; matrix products, arithmetic and copies ran while one was open for 0% -> 0% of each run, Pallas kernels for 16% -> 17%
where the time goes in v6:
time: 29.4 us; the launch traced here: 29.1 us
  starting transfers between devices  16.1 us (55%)
  Pallas kernels  8.29 us (28%)
  waiting for transfers between devices  4.7 us (16%)
    ppermute x2, starting transfers between devices, in_row(): lax.ppermute(block, 'ctx', [(i, i // ROW * ROW + places[i % ROW]) for i i...  8.55 us
    ppermute x2, starting transfers between devices, ahead(): lax.ppermute(block, 'ctx', [(i, i + distance) for i in range(size - dista...  7.52 us
    pallas_call x3, Pallas kernels, attend(): pl.pallas_call(functools.partial(kernel, slots=slots, groups=groups, rows...  5.97 us
    ppermute x2, waiting for transfers between devices, ahead(): lax.ppermute(block, 'ctx', [(i, i + distance) for i in range(size - dista...  4.52 us
    pallas_call x1, Pallas kernels, setup(): pl.pallas_call(functools.partial(setup_kernel, groups=groups, rows=rows,...  1.27 us
    pallas_call x1, Pallas kernels, join(): pl.pallas_call(join_kernel, in_specs=[pl.BlockSpec(memory_space=pltpu.HBM...  0.98 us
  transfers between devices with their start and end apart: 4, of which 2 were waited for; matrix products, arithmetic and copies ran while one was open for 0% of the time, Pallas kernels for 17%

profile of v6, /device:TPU:288, one launch (start us, length us, event | category | flops | bytes accessed | tf_op | source)
XLA Modules:
  0.0 29.1 jit_solution(5989183280392065271)
XLA Ops:
  0.0 1.0 %shard_map.56.own.refs_2_ = bf16[128,1024]{1,0:T(8,128)(2,1)S(1)} custom-call(bf16[128,512]{1,0:T(8,128)(2,1)} %keys.1, bf16[128,512]{1,0:T(8,128)(2,1)} %values.1), custom_call_target="tpu_custom_call" | custom-call | tf_op jit(solution)/shard_map/pallas_call | solution.py:35
  1.0 2.6 %collective-permute-start = (bf16[128,1024]{1,0:T(8,128)(2,1)S(1)}, bf16[128,1024]{1,0:T(8,128)(2,1)S(1)}, u32[]{:S(2)}, u32[]{:S(2)}) collective-permute-start(bf16[128,1024]{1,0:T(8,128)(2,1)S(1)} %shard_map.56.own.refs_2_), channel_id=1, source_target_pairs={{0,32},{8,40},{16,48},{24,56},{32,64},{40,72},{48,80},{56,88},{64,... | collective-permute-start | bytes 786440 | tf_op jit(solution)/shard_map/ppermute | solution.py:278
  3.6 4.9 %collective-permute-start.3 = (bf16[128,1024]{1,0:T(8,128)(2,1)S(1)}, bf16[128,1024]{1,0:T(8,128)(2,1)S(1)}, u32[]{:S(2)}, u32[]{:S(2)}) collective-permute-start(bf16[128,1024]{1,0:T(8,128)(2,1)S(1)} %shard_map.56.own.refs_2_), channel_id=1, source_target_pairs={{0,16},{8,24},{16,32},{24,40},{32,48},{40,56},{48,64},{56,72},{64,... | collective-permute-start | bytes 786440 | tf_op jit(solution)/shard_map/ppermute | solution.py:278
  8.5 4.5 %collective-permute-done.far.refs_3_ = bf16[128,1024]{1,0:T(8,128)(2,1)S(1)} collective-permute-done((bf16[128,1024]{1,0:T(8,128)(2,1)S(1)}, bf16[128,1024]{1,0:T(8,128)(2,1)S(1)}, u32[]{:S(2)}, u32[]{:S(2)}) %collective-permute-start) | collective-permute-done | bytes 262176 | tf_op jit(solution)/shard_map/ppermute | solution.py:278
  13.0 0.1 shard_map.57
  13.1 3.4 %collective-permute-start.2 = (bf16[128,1024]{1,0:T(8,128)(2,1)S(1)}, bf16[128,1024]{1,0:T(8,128)(2,1)S(1)}, u32[]{:S(2)}, u32[]{:S(2)}) collective-permute-start(bf16[128,1024]{1,0:T(8,128)(2,1)S(1)} %get-tuple-element.16), channel_id=1, source_target_pairs={{0,8},{8,0},{16,24},{24,16},{32,40},{40,32},{48,56},{56,48},{64,72... | collective-permute-start | bytes 786440 | tf_op jit(solution)/shard_map/ppermute | solution.py:283
  16.5 5.2 %collective-permute-start.1 = (bf16[128,1024]{1,0:T(8,128)(2,1)S(1)}, bf16[128,1024]{1,0:T(8,128)(2,1)S(1)}, u32[]{:S(2)}, u32[]{:S(2)}) collective-permute-start(bf16[128,1024]{1,0:T(8,128)(2,1)S(1)} %get-tuple-element.15), channel_id=1, source_target_pairs={{0,24},{8,16},{16,8},{24,0},{32,56},{40,48},{48,40},{56,32},{64,88... | collective-permute-start | bytes 786440 | tf_op jit(solution)/shard_map/ppermute | solution.py:283
  21.7 1.3 %shard_map.55 = (f32[5,168,128]{2,1,0:T(8,128)S(1)}, bf16[128,4096]{1,0:T(8,128)(2,1)S(1)}) custom-call(s32[32]{0:T(128)} %docs_far.1, f32[2,4,256]{2,1,0:T(4,128)} %bitcast.1, bf16[128,4096]{1,0:T(8,128)(2,1)} %queries.1), custom_call_target="tpu_custom_call" | custom-call | tf_op jit(solution)/shard_map/pallas_call | solution.py:113
  23.0 0.0 collective-permute-done.3.refs_4_
  23.0 2.4 %shard_map.58 = (f32[4096,128]{1,0:T(8,128)S(1)}, f32[64,128]{1,0:T(8,128)S(1)}) custom-call(f32[5,168,128]{2,1,0:T(8,128)S(1)} %get-tuple-element.13.refs_0_, bf16[128,4096]{1,0:T(8,128)(2,1)S(1)} %get-tuple-element.14.refs_1_, bf16[128,1024]{1,0:T(8,128)(2,1)S(1)} %shard_map.56.own.refs_2_, bf16[128,1024]{1,0:T(8,128)(2,1)S(1)} %collective-permute-done.far.refs_3_, ...), custom_call_target="tpu_custom_call" | custom-call | flops 805306368 | bytes 2097152 | tf_op jit(solution)/shard_map/pallas_call | solution.py:263
  25.4 0.0 collective-permute-done.2.refs_2_
  25.4 1.2 %shard_map.59 = (f32[4096,128]{1,0:T(8,128)S(1)}, f32[64,128]{1,0:T(8,128)S(1)}) custom-call(f32[5,168,128]{2,1,0:T(8,128)S(1)} %get-tuple-element.13.refs_0_, bf16[128,4096]{1,0:T(8,128)(2,1)S(1)} %get-tuple-element.14.refs_1_, bf16[128,1024]{1,0:T(8,128)(2,1)S(1)} %collective-permute-done.2.refs_2_, f32[4096,128]{1,0:T(8,128)S(1)} %get-tuple-element.17.refs_3_, ...), custom_call_target="tpu_custom_call" | custom-call | flops 268435456 | bytes 2097152 | tf_op jit(solution)/shard_map/pallas_call | solution.py:263
  26.7 0.2 collective-permute-done.1.refs_2_
  26.8 2.3 %shard_map.60 = bf16[128,4096]{1,0:T(8,128)(2,1)} custom-call(f32[5,168,128]{2,1,0:T(8,128)S(1)} %get-tuple-element.13.refs_0_, bf16[128,4096]{1,0:T(8,128)(2,1)S(1)} %get-tuple-element.14.refs_1_, bf16[128,1024]{1,0:T(8,128)(2,1)S(1)} %collective-permute-done.1.refs_2_, f32[4096,128]{1,0:T(8,128)S(1)} %get-tuple-element.19.refs_3_, ...), custom_call_target="tpu_custom_call" | custom-call | flops 268435456 | bytes 2097152 | tf_op jit(solution)/shard_map/pallas_call | solution.py:263
Async XLA Ops:
  1.0 12.0 %collective-permute-start = (bf16[128,1024]{1,0:T(8,128)(2,1)S(1)}, bf16[128,1024]{1,0:T(8,128)(2,1)S(1)}, u32[]{:S(2)}, u32[]{:S(2)}) collective-permute-start(bf16[128,1024]{1,0:T(8,128)(2,1)S(1)} %shard_map.56.own.refs_2_), channel_id=1, source_target_pairs={{0,32},{8,40},{16,48},{24,56},{32,64},{40,72},{48,80},{56,88},{64,... | collective-permute-start | bytes 786440 | tf_op jit(solution)/shard_map/ppermute | solution.py:278
  3.6 19.4 %collective-permute-start.3 = (bf16[128,1024]{1,0:T(8,128)(2,1)S(1)}, bf16[128,1024]{1,0:T(8,128)(2,1)S(1)}, u32[]{:S(2)}, u32[]{:S(2)}) collective-permute-start(bf16[128,1024]{1,0:T(8,128)(2,1)S(1)} %shard_map.56.own.refs_2_), channel_id=1, source_target_pairs={{0,16},{8,24},{16,32},{24,40},{32,48},{40,56},{48,64},{56,72},{64,... | collective-permute-start | bytes 786440 | tf_op jit(solution)/shard_map/ppermute | solution.py:278
  13.1 12.3 %collective-permute-start.2 = (bf16[128,1024]{1,0:T(8,128)(2,1)S(1)}, bf16[128,1024]{1,0:T(8,128)(2,1)S(1)}, u32[]{:S(2)}, u32[]{:S(2)}) collective-permute-start(bf16[128,1024]{1,0:T(8,128)(2,1)S(1)} %get-tuple-element.16), channel_id=1, source_target_pairs={{0,8},{8,0},{16,24},{24,16},{32,40},{40,32},{48,56},{56,48},{64,72... | collective-permute-start | bytes 786440 | tf_op jit(solution)/shard_map/ppermute | solution.py:283
  16.5 10.3 %collective-permute-start.1 = (bf16[128,1024]{1,0:T(8,128)(2,1)S(1)}, bf16[128,1024]{1,0:T(8,128)(2,1)S(1)}, u32[]{:S(2)}, u32[]{:S(2)}) collective-permute-start(bf16[128,1024]{1,0:T(8,128)(2,1)S(1)} %get-tuple-element.15), channel_id=1, source_target_pairs={{0,24},{8,16},{16,8},{24,0},{32,56},{40,48},{48,40},{56,32},{64,88... | collective-permute-start | bytes 786440 | tf_op jit(solution)/shard_map/ppermute | solution.py:283

commit v7 on v6

--- a/solution.py
+++ b/solution.py
@@ -160,17 +160,13 @@
                 source = pl.ds(piece * SCALE_BLOCK, SCALE_BLOCK)
                 target = pl.ds(slot * rows + piece * SCALE_BLOCK, SCALE_BLOCK)
                 base = rows + 2 * groups * piece + group
-                kscale = table[slots[slot], base : base + 1, :]
-                scaled = blocks[slot][source, group * HEAD : (group + 1) * HEAD].astype(jnp.float32) * kscale
-                high = scaled.astype(jnp.bfloat16)
-                kparts[at, target, :HEAD] = high
-                kparts[at, target, HEAD:] = (scaled - high.astype(jnp.float32)).astype(jnp.bfloat16)
                 bias[at, target, :] = table[slots[slot], source, :] + table[slots[slot], base + groups : base + groups + 1, :]
             base = rows + 2 * groups * pieces + groups + group
             inverse = table[slots[slot], base : base + 1, :]
             high = inverse.astype(jnp.bfloat16).astype(jnp.float32)
             ones = jnp.where(deep == 0, high, jnp.where(deep == 1, inverse - high, 0.0))
             columns = pl.ds(slot * rows, rows)
+            kparts[at, columns, :] = blocks[slot][:, group * HEAD : (group + 1) * HEAD]
             vparts[at, :HEAD, columns] = blocks[slot][:, (groups + group) * HEAD : (groups + group + 1) * HEAD].T
             vparts[at, HEAD:, columns] = ones.astype(jnp.bfloat16)
 
@@ -188,9 +184,14 @@
         if step * chunk % per == 0:
             prepare(group)
         query = jnp.concatenate([queries[:, h * HEAD : (h + 1) * HEAD] for h in some(step)], axis=0)
-        query = jnp.concatenate([query, query], axis=1)
         score = lax.dot_general(kparts[group % 3], query, LAST, preferred_element_type=jnp.float32)
-        score = score + jnp.concatenate([bias[group % 3]] * chunk, axis=1)
+        scaled = []
+        for at in range(count * pieces):
+            base = rows + 2 * groups * (at % pieces) + group
+            kscale = jnp.concatenate([table[slots[at // pieces], base : base + 1, :]] * chunk, axis=1)
+            keys = slice(at * SCALE_BLOCK, (at + 1) * SCALE_BLOCK)
+            scaled.append(score[keys] * kscale + jnp.concatenate([bias[group % 3, keys, :]] * chunk, axis=1))
+        score = jnp.concatenate(scaled, axis=0)
         scores[step % 2] = score
         top = jnp.max(score, axis=0, keepdims=True)
         if state:
@@ -219,7 +220,7 @@
         for at, h in enumerate(some(step)):
             lanes = slice(at * rows, (at + 1) * rows)
             if final:
-                stage[:, h * HEAD : (h + 1) * HEAD] = result[:, lanes].T.astype(jnp.bfloat16)
+                stage[:, h * HEAD : (h + 1) * HEAD] = result[:, lanes].astype(jnp.bfloat16).T
             else:
                 acc_out[h * HEAD : (h + 1) * HEAD, :] = result[:, lanes]
                 stat_out[h : h + 1, :] = tops[step][:, lanes]
@@ -253,7 +254,7 @@
     scratch = []
     scratch += [
         pltpu.VMEM((3, span, rows), jnp.float32),
-        pltpu.VMEM((3, span, 2 * HEAD), jnp.bfloat16),
+        pltpu.VMEM((3, span, HEAD), jnp.bfloat16),
         pltpu.VMEM((3, HEAD + EXTRA, span), jnp.bfloat16),
         pltpu.VMEM((2, span, chunk * rows), jnp.float32),
         pltpu.VMEM((2, span, chunk * rows), jnp.bfloat16),

time: 29.4 us -> 29.2 us (level)
  no operation moved by 1% of the time
where the time goes in v7:
time: 29.2 us; the launch traced here: 29 us
  starting transfers between devices  16.1 us (55%)
  Pallas kernels  8.13 us (28%)
  waiting for transfers between devices  4.67 us (16%)
    ppermute x2, starting transfers between devices, in_row(): lax.ppermute(block, 'ctx', [(i, i // ROW * ROW + places[i % ROW]) for i i...  8.55 us
    ppermute x2, starting transfers between devices, ahead(): lax.ppermute(block, 'ctx', [(i, i + distance) for i in range(size - dista...  7.52 us
    pallas_call x3, Pallas kernels, attend(): pl.pallas_call(functools.partial(kernel, slots=slots, groups=groups, rows...  5.81 us
    ppermute x2, waiting for transfers between devices, ahead(): lax.ppermute(block, 'ctx', [(i, i + distance) for i in range(size - dista...  4.52 us
    pallas_call x1, Pallas kernels, setup(): pl.pallas_call(functools.partial(setup_kernel, groups=groups, rows=rows,...  1.27 us
    pallas_call x1, Pallas kernels, join(): pl.pallas_call(join_kernel, in_specs=[pl.BlockSpec(memory_space=pltpu.HBM...  0.98 us
  transfers between devices with their start and end apart: 4, of which 2 were waited for; matrix products, arithmetic and copies ran while one was open for 0% of the time, Pallas kernels for 17%

profile of v7, /device:TPU:288, one launch (start us, length us, event | category | flops | bytes accessed | tf_op | source)
XLA Modules:
  0.0 29.0 jit_solution(9909847305107761882)
XLA Ops:
  0.0 1.0 %shard_map.56.own.refs_2_ = bf16[128,1024]{1,0:T(8,128)(2,1)S(1)} custom-call(bf16[128,512]{1,0:T(8,128)(2,1)} %keys.1, bf16[128,512]{1,0:T(8,128)(2,1)} %values.1), custom_call_target="tpu_custom_call" | custom-call | tf_op jit(solution)/shard_map/pallas_call | solution.py:35
  1.0 2.6 %collective-permute-start = (bf16[128,1024]{1,0:T(8,128)(2,1)S(1)}, bf16[128,1024]{1,0:T(8,128)(2,1)S(1)}, u32[]{:S(2)}, u32[]{:S(2)}) collective-permute-start(bf16[128,1024]{1,0:T(8,128)(2,1)S(1)} %shard_map.56.own.refs_2_), channel_id=1, source_target_pairs={{0,32},{8,40},{16,48},{24,56},{32,64},{40,72},{48,80},{56,88},{64,... | collective-permute-start | bytes 786440 | tf_op jit(solution)/shard_map/ppermute | solution.py:279
  3.6 4.9 %collective-permute-start.3 = (bf16[128,1024]{1,0:T(8,128)(2,1)S(1)}, bf16[128,1024]{1,0:T(8,128)(2,1)S(1)}, u32[]{:S(2)}, u32[]{:S(2)}) collective-permute-start(bf16[128,1024]{1,0:T(8,128)(2,1)S(1)} %shard_map.56.own.refs_2_), channel_id=1, source_target_pairs={{0,16},{8,24},{16,32},{24,40},{32,48},{40,56},{48,64},{56,72},{64,... | collective-permute-start | bytes 786440 | tf_op jit(solution)/shard_map/ppermute | solution.py:279
  8.5 4.5 %collective-permute-done.far.refs_3_ = bf16[128,1024]{1,0:T(8,128)(2,1)S(1)} collective-permute-done((bf16[128,1024]{1,0:T(8,128)(2,1)S(1)}, bf16[128,1024]{1,0:T(8,128)(2,1)S(1)}, u32[]{:S(2)}, u32[]{:S(2)}) %collective-permute-start) | collective-permute-done | bytes 262176 | tf_op jit(solution)/shard_map/ppermute | solution.py:279
  13.0 0.1 shard_map.57
  13.1 3.4 %collective-permute-start.2 = (bf16[128,1024]{1,0:T(8,128)(2,1)S(1)}, bf16[128,1024]{1,0:T(8,128)(2,1)S(1)}, u32[]{:S(2)}, u32[]{:S(2)}) collective-permute-start(bf16[128,1024]{1,0:T(8,128)(2,1)S(1)} %get-tuple-element.16), channel_id=1, source_target_pairs={{0,8},{8,0},{16,24},{24,16},{32,40},{40,32},{48,56},{56,48},{64,72... | collective-permute-start | bytes 786440 | tf_op jit(solution)/shard_map/ppermute | solution.py:284
  16.5 5.2 %collective-permute-start.1 = (bf16[128,1024]{1,0:T(8,128)(2,1)S(1)}, bf16[128,1024]{1,0:T(8,128)(2,1)S(1)}, u32[]{:S(2)}, u32[]{:S(2)}) collective-permute-start(bf16[128,1024]{1,0:T(8,128)(2,1)S(1)} %get-tuple-element.15), channel_id=1, source_target_pairs={{0,24},{8,16},{16,8},{24,0},{32,56},{40,48},{48,40},{56,32},{64,88... | collective-permute-start | bytes 786440 | tf_op jit(solution)/shard_map/ppermute | solution.py:284
  21.7 1.3 %shard_map.55 = (f32[5,168,128]{2,1,0:T(8,128)S(1)}, bf16[128,4096]{1,0:T(8,128)(2,1)S(1)}) custom-call(s32[32]{0:T(128)} %docs_far.1, f32[2,4,256]{2,1,0:T(4,128)} %bitcast.1, bf16[128,4096]{1,0:T(8,128)(2,1)} %queries.1), custom_call_target="tpu_custom_call" | custom-call | tf_op jit(solution)/shard_map/pallas_call | solution.py:113
  23.0 0.0 collective-permute-done.3.refs_4_
  23.0 2.6 %shard_map.58 = (f32[4096,128]{1,0:T(8,128)S(1)}, f32[64,128]{1,0:T(8,128)S(1)}) custom-call(f32[5,168,128]{2,1,0:T(8,128)S(1)} %get-tuple-element.13.refs_0_, bf16[128,4096]{1,0:T(8,128)(2,1)S(1)} %get-tuple-element.14.refs_1_, bf16[128,1024]{1,0:T(8,128)(2,1)S(1)} %shard_map.56.own.refs_2_, bf16[128,1024]{1,0:T(8,128)(2,1)S(1)} %collective-permute-done.far.refs_3_, ...), custom_call_target="tpu_custom_call" | custom-call | flops 805306368 | bytes 2097152 | tf_op jit(solution)/shard_map/pallas_call | solution.py:264
  25.5 0.0 collective-permute-done.2.refs_2_
  25.5 1.1 %shard_map.59 = (f32[4096,128]{1,0:T(8,128)S(1)}, f32[64,128]{1,0:T(8,128)S(1)}) custom-call(f32[5,168,128]{2,1,0:T(8,128)S(1)} %get-tuple-element.13.refs_0_, bf16[128,4096]{1,0:T(8,128)(2,1)S(1)} %get-tuple-element.14.refs_1_, bf16[128,1024]{1,0:T(8,128)(2,1)S(1)} %collective-permute-done.2.refs_2_, f32[4096,128]{1,0:T(8,128)S(1)} %get-tuple-element.17.refs_3_, ...), custom_call_target="tpu_custom_call" | custom-call | flops 268435456 | bytes 2097152 | tf_op jit(solution)/shard_map/pallas_call | solution.py:264
  26.7 0.1 collective-permute-done.1.refs_2_
  26.8 2.1 %shard_map.60 = bf16[128,4096]{1,0:T(8,128)(2,1)} custom-call(f32[5,168,128]{2,1,0:T(8,128)S(1)} %get-tuple-element.13.refs_0_, bf16[128,4096]{1,0:T(8,128)(2,1)S(1)} %get-tuple-element.14.refs_1_, bf16[128,1024]{1,0:T(8,128)(2,1)S(1)} %collective-permute-done.1.refs_2_, f32[4096,128]{1,0:T(8,128)S(1)} %get-tuple-element.19.refs_3_, ...), custom_call_target="tpu_custom_call" | custom-call | flops 268435456 | bytes 2097152 | tf_op jit(solution)/shard_map/pallas_call | solution.py:264
Async XLA Ops:
  1.0 12.0 %collective-permute-start = (bf16[128,1024]{1,0:T(8,128)(2,1)S(1)}, bf16[128,1024]{1,0:T(8,128)(2,1)S(1)}, u32[]{:S(2)}, u32[]{:S(2)}) collective-permute-start(bf16[128,1024]{1,0:T(8,128)(2,1)S(1)} %shard_map.56.own.refs_2_), channel_id=1, source_target_pairs={{0,32},{8,40},{16,48},{24,56},{32,64},{40,72},{48,80},{56,88},{64,... | collective-permute-start | bytes 786440 | tf_op jit(solution)/shard_map/ppermute | solution.py:279
  3.6 19.4 %collective-permute-start.3 = (bf16[128,1024]{1,0:T(8,128)(2,1)S(1)}, bf16[128,1024]{1,0:T(8,128)(2,1)S(1)}, u32[]{:S(2)}, u32[]{:S(2)}) collective-permute-start(bf16[128,1024]{1,0:T(8,128)(2,1)S(1)} %shard_map.56.own.refs_2_), channel_id=1, source_target_pairs={{0,16},{8,24},{16,32},{24,40},{32,48},{40,56},{48,64},{56,72},{64,... | collective-permute-start | bytes 786440 | tf_op jit(solution)/shard_map/ppermute | solution.py:279
  13.1 12.4 %collective-permute-start.2 = (bf16[128,1024]{1,0:T(8,128)(2,1)S(1)}, bf16[128,1024]{1,0:T(8,128)(2,1)S(1)}, u32[]{:S(2)}, u32[]{:S(2)}) collective-permute-start(bf16[128,1024]{1,0:T(8,128)(2,1)S(1)} %get-tuple-element.16), channel_id=1, source_target_pairs={{0,8},{8,0},{16,24},{24,16},{32,40},{40,32},{48,56},{56,48},{64,72... | collective-permute-start | bytes 786440 | tf_op jit(solution)/shard_map/ppermute | solution.py:284
  16.5 10.3 %collective-permute-start.1 = (bf16[128,1024]{1,0:T(8,128)(2,1)S(1)}, bf16[128,1024]{1,0:T(8,128)(2,1)S(1)}, u32[]{:S(2)}, u32[]{:S(2)}) collective-permute-start(bf16[128,1024]{1,0:T(8,128)(2,1)S(1)} %get-tuple-element.15), channel_id=1, source_target_pairs={{0,24},{8,16},{16,8},{24,0},{32,56},{40,48},{48,40},{56,32},{64,88... | collective-permute-start | bytes 786440 | tf_op jit(solution)/shard_map/ppermute | solution.py:284

commit v8 on v7

--- a/solution.py
+++ b/solution.py
@@ -60,8 +60,8 @@
     )(own, far)
 
 
-def setup_kernel(docs_far, scales_far, queries, table, near, docs, scales, sems, *, groups, rows, backs):
-    pairs = ((docs_far, docs), (scales_far, scales), (queries, near))
+def setup_kernel(docs_far, scales_far, queries, own, table, near, again, docs, scales, sems, *, groups, rows, backs):
+    pairs = ((docs_far, docs), (scales_far, scales), (own, again), (queries, near))
     copies = [pltpu.make_async_copy(source, target, sems.at[at]) for at, (source, target) in enumerate(pairs)]
     for copy in copies:
         copy.start()
@@ -103,28 +103,30 @@
         at = rows + 2 * groups * pieces
         table[slot, at : at + 2 * groups, :] = 1.0 / line
     copies[2].wait()
-
-
-def setup(docs, scales, queries, groups, backs):
+    copies[3].wait()
+
+
+def setup(docs, scales, queries, own, groups, backs):
     rows = queries.shape[0]
     depth = rows + 2 * groups * (rows // SCALE_BLOCK + 1)
     scales = scales.transpose(1, 2, 0)
     far = [pltpu.with_memory_space_constraint(x, pltpu.HBM) for x in (docs, scales, queries)]
     return pl.pallas_call(
         functools.partial(setup_kernel, groups=groups, rows=rows, backs=backs),
-        in_specs=[pl.BlockSpec(memory_space=pltpu.HBM)] * 3,
-        out_specs=[pl.BlockSpec(memory_space=pltpu.VMEM)] * 2,
+        in_specs=[pl.BlockSpec(memory_space=pltpu.HBM)] * 3 + [pl.BlockSpec(memory_space=pltpu.VMEM)],
+        out_specs=[pl.BlockSpec(memory_space=pltpu.VMEM)] * 3,
         out_shape=[
             pltpu.VMEM((len(backs), depth, rows), jnp.float32),
             pltpu.VMEM(queries.shape, queries.dtype),
+            pltpu.VMEM(own.shape, own.dtype),
         ],
         scratch_shapes=[
             pltpu.SMEM(docs.shape, docs.dtype),
             pltpu.VMEM(scales.shape, scales.dtype),
-            pltpu.SemaphoreType.DMA((3,)),
+            pltpu.SemaphoreType.DMA((4,)),
         ],
         compiler_params=pltpu.CompilerParams(vmem_limit_bytes=4 * 2**20),
-    )(*far)
+    )(*far, own)
 
 
 def kernel(*refs, slots, groups, rows, state, final, chunk):
@@ -288,12 +290,12 @@
     groups = key_value_scales.shape[2]
     own = join(keys, values)
     fourth = ahead(own, 4)
-    second = ahead(own, 2)
+    backs = ((0, 0), (4, 4), (2, 2), (3, 1), (1, 3))
+    table, near, again = setup(doc_lengths, key_value_scales, queries, own, groups, backs)
+    second = ahead(again, 2)
     inner, outer = pick(own, fourth)
     inner = in_row(inner, (1, 0, 3, 2))
     outer = in_row(outer, (3, 2, 1, 0))
-    backs = ((0, 0), (4, 4), (2, 2), (3, 1), (1, 3))
-    table, near = setup(doc_lengths, key_value_scales, queries, groups, backs)
     state = attend(table, near, (own, fourth, second), groups, (0, 1, 2), final=False)
     state = attend(table, near, (inner,), groups, (3,), state=state, final=False)
     return attend(table, near, (outer,), groups, (4,), state=state)

time: 29.2 us -> 29.2 us (level)
    ppermute x2, waiting for transfers between devices: 0.15 us -> 1.45 us  [in_row(): lax.ppermute(block, 'ctx', [(i, i // ROW * ROW + places[i % ROW]) for i i...]
    ppermute x2, waiting for transfers between devices: 4.52 us -> 3.22 us  [ahead(): lax.ppermute(block, 'ctx', [(i, i + distance) for i in range(size - dista...]
where the time goes in v8:
time: 29.2 us; the launch traced here: 29 us
  starting transfers between devices  16.1 us (55%)
  Pallas kernels  8.12 us (28%)
  waiting for transfers between devices  4.68 us (16%)
    ppermute x2, starting transfers between devices, in_row(): lax.ppermute(block, 'ctx', [(i, i // ROW * ROW + places[i % ROW]) for i i...  8.55 us
    ppermute x2, starting transfers between devices, ahead(): lax.ppermute(block, 'ctx', [(i, i + distance) for i in range(size - dista...  7.52 us
    pallas_call x3, Pallas kernels, attend(): pl.pallas_call(functools.partial(kernel, slots=slots, groups=groups, rows...  5.79 us
    ppermute x2, waiting for transfers between devices, ahead(): lax.ppermute(block, 'ctx', [(i, i + distance) for i in range(size - dista...  3.22 us
    ppermute x2, waiting for transfers between devices, in_row(): lax.ppermute(block, 'ctx', [(i, i // ROW * ROW + places[i % ROW]) for i i...  1.45 us
    pallas_call x1, Pallas kernels, setup(): pl.pallas_call(functools.partial(setup_kernel, groups=groups, rows=rows,...  1.29 us
    pallas_call x1, Pallas kernels, join(): pl.pallas_call(join_kernel, in_specs=[pl.BlockSpec(memory_space=pltpu.HBM...  0.98 us
  transfers between devices with their start and end apart: 4, of which 2 were waited for; matrix products, arithmetic and copies ran while one was open for 0% of the time, Pallas kernels for 17%

profile of v8, /device:TPU:288, one launch (start us, length us, event | category | flops | bytes accessed | tf_op | source)
XLA Modules:
  0.0 29.0 jit_solution(15773982241818350706)
XLA Ops:
  0.0 1.0 %shard_map.55.own.refs_2_ = bf16[128,1024]{1,0:T(8,128)(2,1)S(1)} custom-call(bf16[128,512]{1,0:T(8,128)(2,1)} %keys.1, bf16[128,512]{1,0:T(8,128)(2,1)} %values.1), custom_call_target="tpu_custom_call" | custom-call | tf_op jit(solution)/shard_map/pallas_call | solution.py:35
  1.0 2.6 %collective-permute-start = (bf16[128,1024]{1,0:T(8,128)(2,1)S(1)}, bf16[128,1024]{1,0:T(8,128)(2,1)S(1)}, u32[]{:S(2)}, u32[]{:S(2)}) collective-permute-start(bf16[128,1024]{1,0:T(8,128)(2,1)S(1)} %shard_map.55.own.refs_2_), channel_id=1, source_target_pairs={{0,32},{8,40},{16,48},{24,56},{32,64},{40,72},{48,80},{56,88},{64,... | collective-permute-start | bytes 786440 | tf_op jit(solution)/shard_map/ppermute | solution.py:281
  3.6 1.3 %shard_map.56 = (f32[5,168,128]{2,1,0:T(8,128)S(1)}, bf16[128,4096]{1,0:T(8,128)(2,1)S(1)}, bf16[128,1024]{1,0:T(8,128)(2,1)S(1)}) custom-call(s32[32]{0:T(128)} %docs_far.1, f32[2,4,256]{2,1,0:T(4,128)} %bitcast.1, bf16[128,4096]{1,0:T(8,128)(2,1)} %queries.1, bf16[128,1024]{1,0:T(8,128)(2,1)S(1)} %shard_map.55.own.refs_2_), custom_call_target="tpu_custom_call" | custom-call | tf_op jit(solution)/shard_map/pallas_call | solution.py:114
  4.9 4.9 %collective-permute-start.3 = (bf16[128,1024]{1,0:T(8,128)(2,1)S(1)}, bf16[128,1024]{1,0:T(8,128)(2,1)S(1)}, u32[]{:S(2)}, u32[]{:S(2)}) collective-permute-start(bf16[128,1024]{1,0:T(8,128)(2,1)S(1)} %get-tuple-element.18), channel_id=1, source_target_pairs={{0,16},{8,24},{16,32},{24,40},{32,48},{40,56},{48,64},{56,72},{64,... | collective-permute-start | bytes 786440 | tf_op jit(solution)/shard_map/ppermute | solution.py:281
  9.8 3.2 %collective-permute-done.far.refs_3_ = bf16[128,1024]{1,0:T(8,128)(2,1)S(1)} collective-permute-done((bf16[128,1024]{1,0:T(8,128)(2,1)S(1)}, bf16[128,1024]{1,0:T(8,128)(2,1)S(1)}, u32[]{:S(2)}, u32[]{:S(2)}) %collective-permute-start) | collective-permute-done | bytes 262176 | tf_op jit(solution)/shard_map/ppermute | solution.py:281
  13.0 0.1 shard_map.57
  13.1 3.4 %collective-permute-start.2 = (bf16[128,1024]{1,0:T(8,128)(2,1)S(1)}, bf16[128,1024]{1,0:T(8,128)(2,1)S(1)}, u32[]{:S(2)}, u32[]{:S(2)}) collective-permute-start(bf16[128,1024]{1,0:T(8,128)(2,1)S(1)} %get-tuple-element.17), channel_id=1, source_target_pairs={{0,8},{8,0},{16,24},{24,16},{32,40},{40,32},{48,56},{56,48},{64,72... | collective-permute-start | bytes 786440 | tf_op jit(solution)/shard_map/ppermute | solution.py:286
  16.5 5.2 %collective-permute-start.1 = (bf16[128,1024]{1,0:T(8,128)(2,1)S(1)}, bf16[128,1024]{1,0:T(8,128)(2,1)S(1)}, u32[]{:S(2)}, u32[]{:S(2)}) collective-permute-start(bf16[128,1024]{1,0:T(8,128)(2,1)S(1)} %get-tuple-element.16), channel_id=1, source_target_pairs={{0,24},{8,16},{16,8},{24,0},{32,56},{40,48},{48,40},{56,32},{64,88... | collective-permute-start | bytes 786440 | tf_op jit(solution)/shard_map/ppermute | solution.py:286
  21.7 0.0 collective-permute-done.3.refs_4_
  21.7 2.5 %shard_map.58 = (f32[4096,128]{1,0:T(8,128)S(1)}, f32[64,128]{1,0:T(8,128)S(1)}) custom-call(f32[5,168,128]{2,1,0:T(8,128)S(1)} %get-tuple-element.14.refs_0_, bf16[128,4096]{1,0:T(8,128)(2,1)S(1)} %get-tuple-element.15.refs_1_, bf16[128,1024]{1,0:T(8,128)(2,1)S(1)} %shard_map.55.own.refs_2_, bf16[128,1024]{1,0:T(8,128)(2,1)S(1)} %collective-permute-done.far.refs_3_, ...), custom_call_target="tpu_custom_call" | custom-call | flops 805306368 | bytes 2097152 | tf_op jit(solution)/shard_map/pallas_call | solution.py:266
  24.2 0.0 collective-permute-done.2.refs_2_
  24.3 1.1 %shard_map.59 = (f32[4096,128]{1,0:T(8,128)S(1)}, f32[64,128]{1,0:T(8,128)S(1)}) custom-call(f32[5,168,128]{2,1,0:T(8,128)S(1)} %get-tuple-element.14.refs_0_, bf16[128,4096]{1,0:T(8,128)(2,1)S(1)} %get-tuple-element.15.refs_1_, bf16[128,1024]{1,0:T(8,128)(2,1)S(1)} %collective-permute-done.2.refs_2_, f32[4096,128]{1,0:T(8,128)S(1)} %get-tuple-element.19.refs_3_, ...), custom_call_target="tpu_custom_call" | custom-call | flops 268435456 | bytes 2097152 | tf_op jit(solution)/shard_map/pallas_call | solution.py:266
  25.4 1.5 %collective-permute-done.1.refs_2_ = bf16[128,1024]{1,0:T(8,128)(2,1)S(1)} collective-permute-done((bf16[128,1024]{1,0:T(8,128)(2,1)S(1)}, bf16[128,1024]{1,0:T(8,128)(2,1)S(1)}, u32[]{:S(2)}, u32[]{:S(2)}) %collective-permute-start.1) | collective-permute-done | bytes 262176 | tf_op jit(solution)/shard_map/ppermute | solution.py:286
  26.8 2.1 %shard_map.60 = bf16[128,4096]{1,0:T(8,128)(2,1)} custom-call(f32[5,168,128]{2,1,0:T(8,128)S(1)} %get-tuple-element.14.refs_0_, bf16[128,4096]{1,0:T(8,128)(2,1)S(1)} %get-tuple-element.15.refs_1_, bf16[128,1024]{1,0:T(8,128)(2,1)S(1)} %collective-permute-done.1.refs_2_, f32[4096,128]{1,0:T(8,128)S(1)} %get-tuple-element.21.refs_3_, ...), custom_call_target="tpu_custom_call" | custom-call | flops 268435456 | bytes 2097152 | tf_op jit(solution)/shard_map/pallas_call | solution.py:266
Async XLA Ops:
  1.0 12.0 %collective-permute-start = (bf16[128,1024]{1,0:T(8,128)(2,1)S(1)}, bf16[128,1024]{1,0:T(8,128)(2,1)S(1)}, u32[]{:S(2)}, u32[]{:S(2)}) collective-permute-start(bf16[128,1024]{1,0:T(8,128)(2,1)S(1)} %shard_map.55.own.refs_2_), channel_id=1, source_target_pairs={{0,32},{8,40},{16,48},{24,56},{32,64},{40,72},{48,80},{56,88},{64,... | collective-permute-start | bytes 786440 | tf_op jit(solution)/shard_map/ppermute | solution.py:281
  4.9 16.8 %collective-permute-start.3 = (bf16[128,1024]{1,0:T(8,128)(2,1)S(1)}, bf16[128,1024]{1,0:T(8,128)(2,1)S(1)}, u32[]{:S(2)}, u32[]{:S(2)}) collective-permute-start(bf16[128,1024]{1,0:T(8,128)(2,1)S(1)} %get-tuple-element.18), channel_id=1, source_target_pairs={{0,16},{8,24},{16,32},{24,40},{32,48},{40,56},{48,64},{56,72},{64,... | collective-permute-start | bytes 786440 | tf_op jit(solution)/shard_map/ppermute | solution.py:281
  13.1 11.1 %collective-permute-start.2 = (bf16[128,1024]{1,0:T(8,128)(2,1)S(1)}, bf16[128,1024]{1,0:T(8,128)(2,1)S(1)}, u32[]{:S(2)}, u32[]{:S(2)}) collective-permute-start(bf16[128,1024]{1,0:T(8,128)(2,1)S(1)} %get-tuple-element.17), channel_id=1, source_target_pairs={{0,8},{8,0},{16,24},{24,16},{32,40},{40,32},{48,56},{56,48},{64,72... | collective-permute-start | bytes 786440 | tf_op jit(solution)/shard_map/ppermute | solution.py:286
  16.5 10.3 %collective-permute-start.1 = (bf16[128,1024]{1,0:T(8,128)(2,1)S(1)}, bf16[128,1024]{1,0:T(8,128)(2,1)S(1)}, u32[]{:S(2)}, u32[]{:S(2)}) collective-permute-start(bf16[128,1024]{1,0:T(8,128)(2,1)S(1)} %get-tuple-element.16), channel_id=1, source_target_pairs={{0,24},{8,16},{16,8},{24,0},{32,56},{40,48},{48,40},{56,32},{64,88... | collective-permute-start | bytes 786440 | tf_op jit(solution)/shard_map/ppermute | solution.py:286

commit v9 on v7

--- a/solution.py
+++ b/solution.py
@@ -14,6 +14,7 @@
 LAST = (((1,), (1,)), ((), ()))
 EXTRA = 16
 CHUNK = 8
+QUERY_COPIES = 4
 ROW = 4
 
 
@@ -61,7 +62,9 @@
 
 
 def setup_kernel(docs_far, scales_far, queries, table, near, docs, scales, sems, *, groups, rows, backs):
-    pairs = ((docs_far, docs), (scales_far, scales), (queries, near))
+    part = rows // QUERY_COPIES
+    strips = [pl.ds(at * part, part) for at in range(QUERY_COPIES)]
+    pairs = [(docs_far, docs), (scales_far, scales)] + [(queries.at[strip], near.at[strip]) for strip in strips]
     copies = [pltpu.make_async_copy(source, target, sems.at[at]) for at, (source, target) in enumerate(pairs)]
     for copy in copies:
         copy.start()
@@ -102,7 +105,8 @@
             line = jnp.where(lane == piece, wide, line)
         at = rows + 2 * groups * pieces
         table[slot, at : at + 2 * groups, :] = 1.0 / line
-    copies[2].wait()
+    for copy in copies[2:]:
+        copy.wait()
 
 
 def setup(docs, scales, queries, groups, backs):
@@ -121,7 +125,7 @@
         scratch_shapes=[
             pltpu.SMEM(docs.shape, docs.dtype),
             pltpu.VMEM(scales.shape, scales.dtype),
-            pltpu.SemaphoreType.DMA((3,)),
+            pltpu.SemaphoreType.DMA((2 + QUERY_COPIES,)),
         ],
         compiler_params=pltpu.CompilerParams(vmem_limit_bytes=4 * 2**20),
     )(*far)

time: 29.2 us -> 29.2 us (level)
  no operation moved by 1% of the time
where the time goes in v9:
time: 29.2 us; the launch traced here: 29 us
  starting transfers between devices  16.1 us (55%)
  Pallas kernels  8.13 us (28%)
  waiting for transfers between devices  4.67 us (16%)
    ppermute x2, starting transfers between devices, in_row(): lax.ppermute(block, 'ctx', [(i, i // ROW * ROW + places[i % ROW]) for i i...  8.55 us
    ppermute x2, starting transfers between devices, ahead(): lax.ppermute(block, 'ctx', [(i, i + distance) for i in range(size - dista...  7.52 us
    pallas_call x3, Pallas kernels, attend(): pl.pallas_call(functools.partial(kernel, slots=slots, groups=groups, rows...  5.82 us
    ppermute x2, waiting for transfers between devices, ahead(): lax.ppermute(block, 'ctx', [(i, i + distance) for i in range(size - dista...  4.52 us
    pallas_call x1, Pallas kernels, setup(): pl.pallas_call(functools.partial(setup_kernel, groups=groups, rows=rows,...  1.26 us
    pallas_call x1, Pallas kernels, join(): pl.pallas_call(join_kernel, in_specs=[pl.BlockSpec(memory_space=pltpu.HBM...  0.98 us
  transfers between devices with their start and end apart: 4, of which 2 were waited for; matrix products, arithmetic and copies ran while one was open for 0% of the time, Pallas kernels for 17%

profile of v9, /device:TPU:288, one launch (start us, length us, event | category | flops | bytes accessed | tf_op | source)
XLA Modules:
  0.0 29.0 jit_solution(8426707771214535000)
XLA Ops:
  0.0 1.0 %shard_map.56.own.refs_2_ = bf16[128,1024]{1,0:T(8,128)(2,1)S(1)} custom-call(bf16[128,512]{1,0:T(8,128)(2,1)} %keys.1, bf16[128,512]{1,0:T(8,128)(2,1)} %values.1), custom_call_target="tpu_custom_call" | custom-call | tf_op jit(solution)/shard_map/pallas_call | solution.py:36
  1.0 2.6 %collective-permute-start = (bf16[128,1024]{1,0:T(8,128)(2,1)S(1)}, bf16[128,1024]{1,0:T(8,128)(2,1)S(1)}, u32[]{:S(2)}, u32[]{:S(2)}) collective-permute-start(bf16[128,1024]{1,0:T(8,128)(2,1)S(1)} %shard_map.56.own.refs_2_), channel_id=1, source_target_pairs={{0,32},{8,40},{16,48},{24,56},{32,64},{40,72},{48,80},{56,88},{64,... | collective-permute-start | bytes 786440 | tf_op jit(solution)/shard_map/ppermute | solution.py:283
  3.6 4.9 %collective-permute-start.3 = (bf16[128,1024]{1,0:T(8,128)(2,1)S(1)}, bf16[128,1024]{1,0:T(8,128)(2,1)S(1)}, u32[]{:S(2)}, u32[]{:S(2)}) collective-permute-start(bf16[128,1024]{1,0:T(8,128)(2,1)S(1)} %shard_map.56.own.refs_2_), channel_id=1, source_target_pairs={{0,16},{8,24},{16,32},{24,40},{32,48},{40,56},{48,64},{56,72},{64,... | collective-permute-start | bytes 786440 | tf_op jit(solution)/shard_map/ppermute | solution.py:283
  8.5 4.5 %collective-permute-done.far.refs_3_ = bf16[128,1024]{1,0:T(8,128)(2,1)S(1)} collective-permute-done((bf16[128,1024]{1,0:T(8,128)(2,1)S(1)}, bf16[128,1024]{1,0:T(8,128)(2,1)S(1)}, u32[]{:S(2)}, u32[]{:S(2)}) %collective-permute-start) | collective-permute-done | bytes 262176 | tf_op jit(solution)/shard_map/ppermute | solution.py:283
  13.0 0.1 shard_map.57
  13.1 3.4 %collective-permute-start.2 = (bf16[128,1024]{1,0:T(8,128)(2,1)S(1)}, bf16[128,1024]{1,0:T(8,128)(2,1)S(1)}, u32[]{:S(2)}, u32[]{:S(2)}) collective-permute-start(bf16[128,1024]{1,0:T(8,128)(2,1)S(1)} %get-tuple-element.16), channel_id=1, source_target_pairs={{0,8},{8,0},{16,24},{24,16},{32,40},{40,32},{48,56},{56,48},{64,72... | collective-permute-start | bytes 786440 | tf_op jit(solution)/shard_map/ppermute | solution.py:288
  16.5 5.2 %collective-permute-start.1 = (bf16[128,1024]{1,0:T(8,128)(2,1)S(1)}, bf16[128,1024]{1,0:T(8,128)(2,1)S(1)}, u32[]{:S(2)}, u32[]{:S(2)}) collective-permute-start(bf16[128,1024]{1,0:T(8,128)(2,1)S(1)} %get-tuple-element.15), channel_id=1, source_target_pairs={{0,24},{8,16},{16,8},{24,0},{32,56},{40,48},{48,40},{56,32},{64,88... | collective-permute-start | bytes 786440 | tf_op jit(solution)/shard_map/ppermute | solution.py:288
  21.7 1.3 %shard_map.55 = (f32[5,168,128]{2,1,0:T(8,128)S(1)}, bf16[128,4096]{1,0:T(8,128)(2,1)S(1)}) custom-call(s32[32]{0:T(128)} %docs_far.1, f32[2,4,256]{2,1,0:T(4,128)} %bitcast.1, bf16[128,4096]{1,0:T(8,128)(2,1)} %queries.1), custom_call_target="tpu_custom_call" | custom-call | tf_op jit(solution)/shard_map/pallas_call | solution.py:117
  22.9 0.0 collective-permute-done.3.refs_4_
  23.0 2.6 %shard_map.58 = (f32[4096,128]{1,0:T(8,128)S(1)}, f32[64,128]{1,0:T(8,128)S(1)}) custom-call(f32[5,168,128]{2,1,0:T(8,128)S(1)} %get-tuple-element.13.refs_0_, bf16[128,4096]{1,0:T(8,128)(2,1)S(1)} %get-tuple-element.14.refs_1_, bf16[128,1024]{1,0:T(8,128)(2,1)S(1)} %shard_map.56.own.refs_2_, bf16[128,1024]{1,0:T(8,128)(2,1)S(1)} %collective-permute-done.far.refs_3_, ...), custom_call_target="tpu_custom_call" | custom-call | flops 805306368 | bytes 2097152 | tf_op jit(solution)/shard_map/pallas_call | solution.py:268
  25.5 0.0 collective-permute-done.2.refs_2_
  25.5 1.1 %shard_map.59 = (f32[4096,128]{1,0:T(8,128)S(1)}, f32[64,128]{1,0:T(8,128)S(1)}) custom-call(f32[5,168,128]{2,1,0:T(8,128)S(1)} %get-tuple-element.13.refs_0_, bf16[128,4096]{1,0:T(8,128)(2,1)S(1)} %get-tuple-element.14.refs_1_, bf16[128,1024]{1,0:T(8,128)(2,1)S(1)} %collective-permute-done.2.refs_2_, f32[4096,128]{1,0:T(8,128)S(1)} %get-tuple-element.17.refs_3_, ...), custom_call_target="tpu_custom_call" | custom-call | flops 268435456 | bytes 2097152 | tf_op jit(solution)/shard_map/pallas_call | solution.py:268
  26.7 0.2 collective-permute-done.1.refs_2_
  26.8 2.1 %shard_map.60 = bf16[128,4096]{1,0:T(8,128)(2,1)} custom-call(f32[5,168,128]{2,1,0:T(8,128)S(1)} %get-tuple-element.13.refs_0_, bf16[128,4096]{1,0:T(8,128)(2,1)S(1)} %get-tuple-element.14.refs_1_, bf16[128,1024]{1,0:T(8,128)(2,1)S(1)} %collective-permute-done.1.refs_2_, f32[4096,128]{1,0:T(8,128)S(1)} %get-tuple-element.19.refs_3_, ...), custom_call_target="tpu_custom_call" | custom-call | flops 268435456 | bytes 2097152 | tf_op jit(solution)/shard_map/pallas_call | solution.py:268
Async XLA Ops:
  1.0 12.0 %collective-permute-start = (bf16[128,1024]{1,0:T(8,128)(2,1)S(1)}, bf16[128,1024]{1,0:T(8,128)(2,1)S(1)}, u32[]{:S(2)}, u32[]{:S(2)}) collective-permute-start(bf16[128,1024]{1,0:T(8,128)(2,1)S(1)} %shard_map.56.own.refs_2_), channel_id=1, source_target_pairs={{0,32},{8,40},{16,48},{24,56},{32,64},{40,72},{48,80},{56,88},{64,... | collective-permute-start | bytes 786440 | tf_op jit(solution)/shard_map/ppermute | solution.py:283
  3.6 19.4 %collective-permute-start.3 = (bf16[128,1024]{1,0:T(8,128)(2,1)S(1)}, bf16[128,1024]{1,0:T(8,128)(2,1)S(1)}, u32[]{:S(2)}, u32[]{:S(2)}) collective-permute-start(bf16[128,1024]{1,0:T(8,128)(2,1)S(1)} %shard_map.56.own.refs_2_), channel_id=1, source_target_pairs={{0,16},{8,24},{16,32},{24,40},{32,48},{40,56},{48,64},{56,72},{64,... | collective-permute-start | bytes 786440 | tf_op jit(solution)/shard_map/ppermute | solution.py:283
  13.1 12.4 %collective-permute-start.2 = (bf16[128,1024]{1,0:T(8,128)(2,1)S(1)}, bf16[128,1024]{1,0:T(8,128)(2,1)S(1)}, u32[]{:S(2)}, u32[]{:S(2)}) collective-permute-start(bf16[128,1024]{1,0:T(8,128)(2,1)S(1)} %get-tuple-element.16), channel_id=1, source_target_pairs={{0,8},{8,0},{16,24},{24,16},{32,40},{40,32},{48,56},{56,48},{64,72... | collective-permute-start | bytes 786440 | tf_op jit(solution)/shard_map/ppermute | solution.py:288
  16.5 10.3 %collective-permute-start.1 = (bf16[128,1024]{1,0:T(8,128)(2,1)S(1)}, bf16[128,1024]{1,0:T(8,128)(2,1)S(1)}, u32[]{:S(2)}, u32[]{:S(2)}) collective-permute-start(bf16[128,1024]{1,0:T(8,128)(2,1)S(1)} %get-tuple-element.15), channel_id=1, source_target_pairs={{0,24},{8,16},{16,8},{24,0},{32,56},{40,48},{48,40},{56,32},{64,88... | collective-permute-start | bytes 786440 | tf_op jit(solution)/shard_map/ppermute | solution.py:288

commit v10 on v9

--- a/solution.py
+++ b/solution.py
@@ -79,7 +79,7 @@
         end = end + docs[doc]
         return end, jnp.where(end <= qpos, end, start)
 
-    _, start = lax.fori_loop(0, docs.shape[0], visit, (0, jnp.zeros((8, rows), jnp.int32)), unroll=8)
+    _, start = lax.fori_loop(0, docs.shape[0], visit, (0, jnp.zeros((8, rows), jnp.int32)), unroll=True)
     both = jnp.concatenate([scales[0], scales[1]], axis=0)
     place = lax.broadcasted_iota(jnp.int32, both.shape, 1)
     lane = lax.broadcasted_iota(jnp.int32, (2 * groups, rows), 1) // SCALE_BLOCK

time: 29.2 us -> 29.2 us (level)
  no operation moved by 1% of the time
where the time goes in v10:
time: 29.2 us; the launch traced here: 29 us
  starting transfers between devices  16.1 us (55%)
  Pallas kernels  8.13 us (28%)
  waiting for transfers between devices  4.67 us (16%)
    ppermute x2, starting transfers between devices, in_row(): lax.ppermute(block, 'ctx', [(i, i // ROW * ROW + places[i % ROW]) for i i...  8.55 us
    ppermute x2, starting transfers between devices, ahead(): lax.ppermute(block, 'ctx', [(i, i + distance) for i in range(size - dista...  7.52 us
    pallas_call x3, Pallas kernels, attend(): pl.pallas_call(functools.partial(kernel, slots=slots, groups=groups, rows...  5.82 us
    ppermute x2, waiting for transfers between devices, ahead(): lax.ppermute(block, 'ctx', [(i, i + distance) for i in range(size - dista...  4.52 us
    pallas_call x1, Pallas kernels, setup(): pl.pallas_call(functools.partial(setup_kernel, groups=groups, rows=rows,...  1.26 us
    pallas_call x1, Pallas kernels, join(): pl.pallas_call(join_kernel, in_specs=[pl.BlockSpec(memory_space=pltpu.HBM...  0.98 us
  transfers between devices with their start and end apart: 4, of which 2 were waited for; matrix products, arithmetic and copies ran while one was open for 0% of the time, Pallas kernels for 17%

profile of v10, /device:TPU:288, one launch (start us, length us, event | category | flops | bytes accessed | tf_op | source)
XLA Modules:
  0.0 29.0 jit_solution(18302093739795385082)
XLA Ops:
  0.0 1.0 %shard_map.56.own.refs_2_ = bf16[128,1024]{1,0:T(8,128)(2,1)S(1)} custom-call(bf16[128,512]{1,0:T(8,128)(2,1)} %keys.1, bf16[128,512]{1,0:T(8,128)(2,1)} %values.1), custom_call_target="tpu_custom_call" | custom-call | tf_op jit(solution)/shard_map/pallas_call | solution.py:36
  1.0 2.6 %collective-permute-start = (bf16[128,1024]{1,0:T(8,128)(2,1)S(1)}, bf16[128,1024]{1,0:T(8,128)(2,1)S(1)}, u32[]{:S(2)}, u32[]{:S(2)}) collective-permute-start(bf16[128,1024]{1,0:T(8,128)(2,1)S(1)} %shard_map.56.own.refs_2_), channel_id=1, source_target_pairs={{0,32},{8,40},{16,48},{24,56},{32,64},{40,72},{48,80},{56,88},{64,... | collective-permute-start | bytes 786440 | tf_op jit(solution)/shard_map/ppermute | solution.py:283
  3.6 4.9 %collective-permute-start.3 = (bf16[128,1024]{1,0:T(8,128)(2,1)S(1)}, bf16[128,1024]{1,0:T(8,128)(2,1)S(1)}, u32[]{:S(2)}, u32[]{:S(2)}) collective-permute-start(bf16[128,1024]{1,0:T(8,128)(2,1)S(1)} %shard_map.56.own.refs_2_), channel_id=1, source_target_pairs={{0,16},{8,24},{16,32},{24,40},{32,48},{40,56},{48,64},{56,72},{64,... | collective-permute-start | bytes 786440 | tf_op jit(solution)/shard_map/ppermute | solution.py:283
  8.5 4.5 %collective-permute-done.far.refs_3_ = bf16[128,1024]{1,0:T(8,128)(2,1)S(1)} collective-permute-done((bf16[128,1024]{1,0:T(8,128)(2,1)S(1)}, bf16[128,1024]{1,0:T(8,128)(2,1)S(1)}, u32[]{:S(2)}, u32[]{:S(2)}) %collective-permute-start) | collective-permute-done | bytes 262176 | tf_op jit(solution)/shard_map/ppermute | solution.py:283
  13.0 0.1 shard_map.57
  13.1 3.4 %collective-permute-start.2 = (bf16[128,1024]{1,0:T(8,128)(2,1)S(1)}, bf16[128,1024]{1,0:T(8,128)(2,1)S(1)}, u32[]{:S(2)}, u32[]{:S(2)}) collective-permute-start(bf16[128,1024]{1,0:T(8,128)(2,1)S(1)} %get-tuple-element.16), channel_id=1, source_target_pairs={{0,8},{8,0},{16,24},{24,16},{32,40},{40,32},{48,56},{56,48},{64,72... | collective-permute-start | bytes 786440 | tf_op jit(solution)/shard_map/ppermute | solution.py:288
  16.5 5.2 %collective-permute-start.1 = (bf16[128,1024]{1,0:T(8,128)(2,1)S(1)}, bf16[128,1024]{1,0:T(8,128)(2,1)S(1)}, u32[]{:S(2)}, u32[]{:S(2)}) collective-permute-start(bf16[128,1024]{1,0:T(8,128)(2,1)S(1)} %get-tuple-element.15), channel_id=1, source_target_pairs={{0,24},{8,16},{16,8},{24,0},{32,56},{40,48},{48,40},{56,32},{64,88... | collective-permute-start | bytes 786440 | tf_op jit(solution)/shard_map/ppermute | solution.py:288
  21.7 1.3 %shard_map.55 = (f32[5,168,128]{2,1,0:T(8,128)S(1)}, bf16[128,4096]{1,0:T(8,128)(2,1)S(1)}) custom-call(s32[32]{0:T(128)} %docs_far.1, f32[2,4,256]{2,1,0:T(4,128)} %bitcast.1, bf16[128,4096]{1,0:T(8,128)(2,1)} %queries.1), custom_call_target="tpu_custom_call" | custom-call | tf_op jit(solution)/shard_map/pallas_call | solution.py:117
  22.9 0.0 collective-permute-done.3.refs_4_
  23.0 2.6 %shard_map.58 = (f32[4096,128]{1,0:T(8,128)S(1)}, f32[64,128]{1,0:T(8,128)S(1)}) custom-call(f32[5,168,128]{2,1,0:T(8,128)S(1)} %get-tuple-element.13.refs_0_, bf16[128,4096]{1,0:T(8,128)(2,1)S(1)} %get-tuple-element.14.refs_1_, bf16[128,1024]{1,0:T(8,128)(2,1)S(1)} %shard_map.56.own.refs_2_, bf16[128,1024]{1,0:T(8,128)(2,1)S(1)} %collective-permute-done.far.refs_3_, ...), custom_call_target="tpu_custom_call" | custom-call | flops 805306368 | bytes 2097152 | tf_op jit(solution)/shard_map/pallas_call | solution.py:268
  25.5 0.0 collective-permute-done.2.refs_2_
  25.5 1.1 %shard_map.59 = (f32[4096,128]{1,0:T(8,128)S(1)}, f32[64,128]{1,0:T(8,128)S(1)}) custom-call(f32[5,168,128]{2,1,0:T(8,128)S(1)} %get-tuple-element.13.refs_0_, bf16[128,4096]{1,0:T(8,128)(2,1)S(1)} %get-tuple-element.14.refs_1_, bf16[128,1024]{1,0:T(8,128)(2,1)S(1)} %collective-permute-done.2.refs_2_, f32[4096,128]{1,0:T(8,128)S(1)} %get-tuple-element.17.refs_3_, ...), custom_call_target="tpu_custom_call" | custom-call | flops 268435456 | bytes 2097152 | tf_op jit(solution)/shard_map/pallas_call | solution.py:268
  26.7 0.2 collective-permute-done.1.refs_2_
  26.8 2.1 %shard_map.60 = bf16[128,4096]{1,0:T(8,128)(2,1)} custom-call(f32[5,168,128]{2,1,0:T(8,128)S(1)} %get-tuple-element.13.refs_0_, bf16[128,4096]{1,0:T(8,128)(2,1)S(1)} %get-tuple-element.14.refs_1_, bf16[128,1024]{1,0:T(8,128)(2,1)S(1)} %collective-permute-done.1.refs_2_, f32[4096,128]{1,0:T(8,128)S(1)} %get-tuple-element.19.refs_3_, ...), custom_call_target="tpu_custom_call" | custom-call | flops 268435456 | bytes 2097152 | tf_op jit(solution)/shard_map/pallas_call | solution.py:268
Async XLA Ops:
  1.0 12.0 %collective-permute-start = (bf16[128,1024]{1,0:T(8,128)(2,1)S(1)}, bf16[128,1024]{1,0:T(8,128)(2,1)S(1)}, u32[]{:S(2)}, u32[]{:S(2)}) collective-permute-start(bf16[128,1024]{1,0:T(8,128)(2,1)S(1)} %shard_map.56.own.refs_2_), channel_id=1, source_target_pairs={{0,32},{8,40},{16,48},{24,56},{32,64},{40,72},{48,80},{56,88},{64,... | collective-permute-start | bytes 786440 | tf_op jit(solution)/shard_map/ppermute | solution.py:283
  3.6 19.4 %collective-permute-start.3 = (bf16[128,1024]{1,0:T(8,128)(2,1)S(1)}, bf16[128,1024]{1,0:T(8,128)(2,1)S(1)}, u32[]{:S(2)}, u32[]{:S(2)}) collective-permute-start(bf16[128,1024]{1,0:T(8,128)(2,1)S(1)} %shard_map.56.own.refs_2_), channel_id=1, source_target_pairs={{0,16},{8,24},{16,32},{24,40},{32,48},{40,56},{48,64},{56,72},{64,... | collective-permute-start | bytes 786440 | tf_op jit(solution)/shard_map/ppermute | solution.py:283
  13.1 12.4 %collective-permute-start.2 = (bf16[128,1024]{1,0:T(8,128)(2,1)S(1)}, bf16[128,1024]{1,0:T(8,128)(2,1)S(1)}, u32[]{:S(2)}, u32[]{:S(2)}) collective-permute-start(bf16[128,1024]{1,0:T(8,128)(2,1)S(1)} %get-tuple-element.16), channel_id=1, source_target_pairs={{0,8},{8,0},{16,24},{24,16},{32,40},{40,32},{48,56},{56,48},{64,72... | collective-permute-start | bytes 786440 | tf_op jit(solution)/shard_map/ppermute | solution.py:288
  16.5 10.3 %collective-permute-start.1 = (bf16[128,1024]{1,0:T(8,128)(2,1)S(1)}, bf16[128,1024]{1,0:T(8,128)(2,1)S(1)}, u32[]{:S(2)}, u32[]{:S(2)}) collective-permute-start(bf16[128,1024]{1,0:T(8,128)(2,1)S(1)} %get-tuple-element.15), channel_id=1, source_target_pairs={{0,24},{8,16},{16,8},{24,0},{32,56},{40,48},{48,40},{56,32},{64,88... | collective-permute-start | bytes 786440 | tf_op jit(solution)/shard_map/ppermute | solution.py:288
